TPU v7x, 32 devices: a whole 2x2x4 slice. The times are simulated.
32 devices in a mesh: dp: 32 (over z, y, x, core).
Axes of the slice: x: 2, y: 2, z: 4, core: 2. Of those that a mesh axis runs over, the one named last changes fastest.
Arguments:
- activations: bfloat16 [65536, 512], P('dp'), may hold values from -6 to 6
- cotangent: float32 [65536, 512], P('dp'), may hold values from -6 to 6
- video_length: int32 [32, 2], replicated, may hold values from 204 to 1024, as said below
- mix_weight: float32 [4, 512, 512], P(None, 'dp'), may hold values from -1.06066017 to 1.06066017
- mix_first: float32 [4, 512, 512], P(None, 'dp'), may hold values from -0.00018310547 to 0.00018310547
- mix_second: float32 [4, 512, 512], P(None, 'dp'), may hold values from 1.373291e-11 to 5.493164e-11
- mix_average: float32 [4, 512, 512], P(None, 'dp'), may hold values from -0.25 to 0.25
- up_weight: float32 [512, 2048], P('dp'), may hold values from -0.25 to 0.25
- up_first: float32 [512, 2048], P('dp'), may hold values from -0.00018310547 to 0.00018310547
- up_second: float32 [512, 2048], P('dp'), may hold values from 1.373291e-11 to 5.493164e-11
- up_average: float32 [512, 2048], P('dp'), may hold values from -0.25 to 0.25
- down_weight: float32 [2048, 512], P('dp'), may hold values from -0.125 to 0.125
- down_first: float32 [2048, 512], P('dp'), may hold values from -0.00018310547 to 0.00018310547
- down_second: float32 [2048, 512], P('dp'), may hold values from 1.373291e-11 to 5.493164e-11
- down_average: float32 [2048, 512], P('dp'), may hold values from -0.125 to 0.125
- vector_weight: float32 [28, 512], P(None, 'dp'), may hold values from -3 to 3
- vector_first: float32 [28, 512], P(None, 'dp'), may hold values from -0.0007324219 to 0.0007324219
- vector_second: float32 [28, 512], P(None, 'dp'), may hold values from 2.1972656e-10 to 8.789062e-10
- vector_average: float32 [28, 512], P(None, 'dp'), may hold values from -4 to 4
Outputs:
- block_output: bfloat16 [65536, 512], P('dp')
- input_grad: float32 [65536, 512], P('dp')
- grad_norm: float32 [], replicated
- new_mix_weight: float32 [4, 512, 512], P(None, 'dp')
- new_mix_first: float32 [4, 512, 512], P(None, 'dp')
- new_mix_second: float32 [4, 512, 512], P(None, 'dp')
- new_mix_average: float32 [4, 512, 512], P(None, 'dp')
- new_up_weight: float32 [512, 2048], P('dp')
- new_up_first: float32 [512, 2048], P('dp')
- new_up_second: float32 [512, 2048], P('dp')
- new_up_average: float32 [512, 2048], P('dp')
- new_down_weight: float32 [2048, 512], P('dp')
- new_down_first: float32 [2048, 512], P('dp')
- new_down_second: float32 [2048, 512], P('dp')
- new_down_average: float32 [2048, 512], P('dp')
- new_vector_weight: float32 [28, 512], P(None, 'dp')
- new_vector_first: float32 [28, 512], P(None, 'dp')
- new_vector_second: float32 [28, 512], P(None, 'dp')
- new_vector_average: float32 [28, 512], P(None, 'dp')
- clipped_bias_grad: float32 [512], P('dp')
Inputs may be any that keep to these rules, and one draw needn't show every extreme that they name: `video_length`: each of the 2 videos of a group has 204 to 1024 frames; in every draw some group holds 2 videos of 1024 frames.
All inputs are finite; a program needn't handle non-finite values.
Results may differ from a plain program's by a relative error of at most 0.007.
The roundings to bfloat16 on the way count: a program that leaves them out, or rounds other values in their place, can miss the bound.
Values may be sent and summed in bfloat16 or wider, within the bound.
A program may use at most 256 MiB of HBM per device.

v0:
```python
import math

import jax
import jax.numpy as jnp
from jax import lax
from jax.sharding import PartitionSpec as P

HEADS = 4
WINDOW = 19
SLOTS = 2
STEP = 10
FRAMES_DEV = 2048
NPARAM = 3160064


def norm_forward(value, gain, shift):
    center = value - jnp.mean(value, axis=-1, keepdims=True)
    scale = lax.rsqrt(jnp.mean(center * center, axis=-1, keepdims=True) + 1e-05)
    normal = center * scale
    return (normal * gain + shift, normal, scale)


def norm_backward(upstream, gain, normal, scale):
    d_gain = jnp.sum(upstream * normal, axis=0)
    d_shift = jnp.sum(upstream, axis=0)
    inner = upstream * gain
    d_value = scale * (
        inner
        - jnp.mean(inner, axis=-1, keepdims=True)
        - normal * jnp.mean(inner * normal, axis=-1, keepdims=True)
    )
    return (d_value, d_gain, d_shift)


def earlier(field, same_prev):
    return jnp.concatenate([jnp.zeros_like(field[:1]), field[:-1]], 0) * same_prev


def later(field, same_next):
    return jnp.concatenate([field[1:], jnp.zeros_like(field[:1])], 0) * same_next


def contract(left, right):
    return jnp.einsum("fi,fj->ij", left, right, preferred_element_type=jnp.float32)


def gelu_exact(value):
    return jax.nn.gelu(value, approximate=False)


def adamw(gradient, weight, moment_one, moment_two, average, rate):
    new_one = 0.9 * moment_one + 0.1 * gradient
    new_two = 0.999 * moment_two + 0.001 * gradient * gradient
    corrected = new_one / (1.0 - 0.9**STEP)
    spread = jnp.sqrt(new_two / (1.0 - 0.999**STEP)) + 1e-08
    new_weight = weight - rate * (corrected / spread + 0.1 * weight)
    new_average = 0.9 * average + 0.1 * new_weight
    return (new_weight, new_one, new_two, new_average)


def body(
    activations,
    cotangent,
    video_length,
    mix_weight,
    mix_first,
    mix_second,
    mix_average,
    up_weight,
    up_first,
    up_second,
    up_average,
    down_weight,
    down_first,
    down_second,
    down_average,
    vector_weight,
    vector_first,
    vector_second,
    vector_average,
):
    groups = lax.axis_size("dp")
    rank = lax.axis_index("dp")
    frames_dev = activations.shape[0]
    model_width = activations.shape[1]
    head_size = model_width // HEADS
    radius = WINDOW // 2
    block_rows = min(512, frames_dev)
    blocks = frames_dev // block_rows
    span = block_rows + 2 * radius
    mixes, up_full, down_full, vectors = (
        lax.all_gather(mix_weight.astype(jnp.bfloat16), "dp", axis=1, tiled=True),
        lax.all_gather(up_weight.astype(jnp.bfloat16), "dp", axis=0, tiled=True),
        lax.all_gather(down_weight.astype(jnp.bfloat16), "dp", axis=0, tiled=True),
        lax.all_gather(vector_weight.astype(jnp.bfloat16), "dp", axis=1, tiled=True),
    )
    vectors = vectors.astype(jnp.float32)
    lengths = lax.dynamic_slice_in_dim(video_length, rank, 1, 0)[0]
    video_ends = jnp.cumsum(lengths)
    places = jnp.arange(frames_dev, dtype=jnp.int32)
    segment = jnp.sum((places[:, None] >= video_ends[None, :]).astype(jnp.int32), axis=1)
    live_mask = (segment < SLOTS).astype(jnp.float32)[:, None]
    same_video = (segment[1:] == segment[:-1]).astype(jnp.float32)
    zero_one = jnp.zeros((1,), jnp.float32)
    same_prev = jnp.concatenate([zero_one, same_video])[:, None]
    same_next = jnp.concatenate([same_video, zero_one])[:, None]
    frames = activations.astype(jnp.float32)
    normed, normal_one, scale_one = norm_forward(frames, vectors[0], vectors[1])
    before = earlier(normed, same_prev)
    after_rows = later(normed, same_next)

    def convolve(first_row):
        return live_mask * (
            vectors[first_row] * before
            + vectors[first_row + 1] * normed
            + vectors[first_row + 2] * after_rows
        )

    q_normed, q_normal, q_scale = norm_forward(convolve(15), vectors[2], vectors[3])
    k_normed, k_normal, k_scale = norm_forward(convolve(18), vectors[4], 0.0)
    v_normed, v_normal, v_scale = norm_forward(convolve(21), vectors[5], vectors[6])
    q_low = q_normed.astype(jnp.bfloat16)
    k_low = k_normed.astype(jnp.bfloat16)
    v_low = v_normed.astype(jnp.bfloat16)
    factor = head_size ** (-0.5)
    query = (
        (jnp.dot(q_low, mixes[0], preferred_element_type=jnp.float32) + vectors[9]) * factor
    ).astype(jnp.bfloat16)
    keys_out = jnp.dot(k_low, mixes[1], preferred_element_type=jnp.float32).astype(jnp.bfloat16)
    values_out = (
        jnp.dot(v_low, mixes[2], preferred_element_type=jnp.float32) + vectors[10]
    ).astype(jnp.bfloat16)
    query_heads = query.reshape(frames_dev, HEADS, head_size)
    key_pad = jnp.pad(
        keys_out.reshape(frames_dev, HEADS, head_size), ((radius, radius), (0, 0), (0, 0))
    )
    value_pad = jnp.pad(
        values_out.reshape(frames_dev, HEADS, head_size), ((radius, radius), (0, 0), (0, 0))
    )
    seg_pad = jnp.pad(segment, (radius, radius), constant_values=-1)
    offset = jnp.arange(span)[None, :] - jnp.arange(block_rows)[:, None]
    in_band = (offset >= 0) & (offset <= 2 * radius)
    starts = jnp.arange(blocks, dtype=jnp.int32) * block_rows

    def scores_of(start):
        query_rows = lax.dynamic_slice_in_dim(query_heads, start, block_rows, 0)
        key_rows = lax.dynamic_slice_in_dim(key_pad, start, span, 0)
        value_rows = lax.dynamic_slice_in_dim(value_pad, start, span, 0)
        seg_rows = lax.dynamic_slice_in_dim(seg_pad, start + radius, block_rows, 0)
        seg_keys = lax.dynamic_slice_in_dim(seg_pad, start, span, 0)
        allowed = (in_band & (seg_rows[:, None] == seg_keys[None, :]))[None]
        scores = jnp.einsum(
            "qhe,khe->hqk", query_rows, key_rows, preferred_element_type=jnp.float32
        )
        return (query_rows, key_rows, value_rows, allowed, scores)

    def attend_forward(start):
        query_rows, key_rows, value_rows, allowed, scores = scores_of(start)
        masked = jnp.where(allowed, scores, -1e30)
        row_top = jnp.max(masked, axis=-1, keepdims=True)
        weights = jnp.exp(masked - row_top) * allowed.astype(jnp.float32)
        totals = jnp.sum(weights, axis=-1, keepdims=True)
        probs = (weights / totals).astype(jnp.bfloat16)
        mixed = jnp.einsum("hqk,khe->qhe", probs, value_rows, preferred_element_type=jnp.float32)
        return (mixed, row_top + jnp.log(totals))

    attended, log_totals = lax.map(attend_forward, starts)
    attended_low = attended.reshape(frames_dev, model_width).astype(jnp.bfloat16)
    projected = jnp.dot(attended_low, mixes[3], preferred_element_type=jnp.float32) + vectors[11]
    middle = frames * live_mask + vectors[13] * live_mask * projected
    normed_two, normal_two, scale_two = norm_forward(middle, vectors[7], vectors[8])
    normed_low = normed_two.astype(jnp.bfloat16)
    hidden_pre = jnp.dot(normed_low, up_full, preferred_element_type=jnp.float32) + vectors[
        24:
    ].reshape(-1)
    hidden_val, gelu_pull = jax.vjp(gelu_exact, hidden_pre)
    hidden_low = hidden_val.astype(jnp.bfloat16)
    mlp_out = jnp.dot(hidden_low, down_full, preferred_element_type=jnp.float32) + vectors[12]
    block_output = (middle + vectors[14] * live_mask * mlp_out).astype(jnp.bfloat16)
    d_mlp = (vectors[14] * live_mask * cotangent).astype(jnp.bfloat16)
    grad_down = contract(hidden_low, d_mlp)
    bias_down = jnp.sum(d_mlp.astype(jnp.float32), axis=0)
    scale_mlp = jnp.sum(cotangent * live_mask * mlp_out, axis=0)
    d_hidden = jnp.einsum("fj,ij->fi", d_mlp, down_full, preferred_element_type=jnp.float32)
    d_pre = gelu_pull(d_hidden)[0].astype(jnp.bfloat16)
    grad_up = contract(normed_low, d_pre)
    bias_up = jnp.sum(d_pre.astype(jnp.float32), axis=0)
    d_normed_two = jnp.einsum("fj,ij->fi", d_pre, up_full, preferred_element_type=jnp.float32)
    d_middle_norm, gain_two, shift_two = norm_backward(
        d_normed_two, vectors[7], normal_two, scale_two
    )
    d_middle = cotangent + d_middle_norm
    d_proj = (vectors[13] * live_mask * d_middle).astype(jnp.bfloat16)
    scale_attn = jnp.sum(d_middle * live_mask * projected, axis=0)
    grad_proj = contract(attended_low, d_proj)
    bias_proj = jnp.sum(d_proj.astype(jnp.float32), axis=0)
    d_attended = jnp.einsum(
        "fj,ij->fi", d_proj, mixes[3], preferred_element_type=jnp.float32
    ).astype(jnp.bfloat16)
    d_attended = d_attended.reshape(frames_dev, HEADS, head_size)

    def attend_back(carry, inputs):
        key_acc, value_acc = carry
        start, log_total = inputs
        query_rows, key_rows, value_rows, allowed, scores = scores_of(start)
        probs = jnp.exp(jnp.where(allowed, scores, -1e30) - log_total) * allowed.astype(jnp.float32)
        grad_rows = lax.dynamic_slice_in_dim(d_attended, start, block_rows, 0)
        d_probs = jnp.einsum(
            "qhe,khe->hqk", grad_rows, value_rows, preferred_element_type=jnp.float32
        )
        inner = jnp.sum(probs * d_probs, axis=-1, keepdims=True)
        d_scores = (probs * (d_probs - inner)).astype(jnp.bfloat16)
        d_query_rows = jnp.einsum(
            "hqk,khe->qhe", d_scores, key_rows, preferred_element_type=jnp.float32
        )
        d_key_rows = jnp.einsum(
            "hqk,qhe->khe", d_scores, query_rows, preferred_element_type=jnp.float32
        )
        d_value_rows = jnp.einsum(
            "hqk,qhe->khe",
            probs.astype(jnp.bfloat16),
            grad_rows,
            preferred_element_type=jnp.float32,
        )
        key_acc = lax.dynamic_update_slice_in_dim(
            key_acc, lax.dynamic_slice_in_dim(key_acc, start, span, 0) + d_key_rows, start, 0
        )
        value_acc = lax.dynamic_update_slice_in_dim(
            value_acc, lax.dynamic_slice_in_dim(value_acc, start, span, 0) + d_value_rows, start, 0
        )
        return ((key_acc, value_acc), d_query_rows)

    zeros_pad = jnp.zeros((frames_dev + 2 * radius, HEADS, head_size), jnp.float32)
    (key_acc, value_acc), d_query_all = lax.scan(
        attend_back, (zeros_pad, zeros_pad), (starts, log_totals)
    )
    d_query = d_query_all.reshape(frames_dev, model_width).astype(jnp.bfloat16)
    d_key = (
        key_acc[radius : radius + frames_dev].reshape(frames_dev, model_width).astype(jnp.bfloat16)
    )
    d_value = (
        value_acc[radius : radius + frames_dev]
        .reshape(frames_dev, model_width)
        .astype(jnp.bfloat16)
    )
    grad_query = factor * contract(q_low, d_query)
    bias_query = factor * jnp.sum(d_query.astype(jnp.float32), axis=0)
    d_q_in = factor * jnp.einsum("fj,ij->fi", d_query, mixes[0], preferred_element_type=jnp.float32)
    grad_key = contract(k_low, d_key)
    d_k_in = jnp.einsum("fj,ij->fi", d_key, mixes[1], preferred_element_type=jnp.float32)
    grad_value = contract(v_low, d_value)
    bias_value = jnp.sum(d_value.astype(jnp.float32), axis=0)
    d_v_in = jnp.einsum("fj,ij->fi", d_value, mixes[2], preferred_element_type=jnp.float32)
    d_conv_q, gain_q, shift_q = norm_backward(d_q_in, vectors[2], q_normal, q_scale)
    d_conv_k, gain_k, shift_k = norm_backward(d_k_in, vectors[4], k_normal, k_scale)
    d_conv_v, gain_v, shift_v = norm_backward(d_v_in, vectors[5], v_normal, v_scale)

    def conv_back(d_conv, first_row):
        masked = d_conv * live_mask
        tap_grads = jnp.stack(
            [
                jnp.sum(masked * before, axis=0),
                jnp.sum(masked * normed, axis=0),
                jnp.sum(masked * after_rows, axis=0),
            ]
        )
        d_normed = (
            vectors[first_row + 1] * masked
            + later(vectors[first_row] * masked, same_next)
            + earlier(vectors[first_row + 2] * masked, same_prev)
        )
        return (d_normed, tap_grads)

    d_from_q, taps_q = conv_back(d_conv_q, 15)
    d_from_k, taps_k = conv_back(d_conv_k, 18)
    d_from_v, taps_v = conv_back(d_conv_v, 21)
    d_normed_one = d_from_q + d_from_k + d_from_v
    d_norm_one, gain_one, shift_one = norm_backward(d_normed_one, vectors[0], normal_one, scale_one)
    input_grad = d_middle * live_mask + d_norm_one
    vector_grad = jnp.concatenate(
        [
            jnp.stack(
                [
                    gain_one,
                    shift_one,
                    gain_q,
                    shift_q,
                    gain_k,
                    gain_v,
                    shift_v,
                    gain_two,
                    shift_two,
                    bias_query,
                    bias_value,
                    bias_proj,
                    bias_down,
                    scale_attn,
                    scale_mlp,
                ]
            ),
            taps_q,
            taps_k,
            taps_v,
            bias_up.reshape(-1, model_width),
        ],
        0,
    )
    mix_grad = jnp.stack([grad_query, grad_key, grad_value, grad_proj])
    live_total = jnp.sum(video_length).astype(jnp.float32)
    shard_width = mix_weight.shape[1]
    shard_hidden = down_weight.shape[0]
    mix_all, up_all, down_all, vector_all = lax.psum(
        (mix_grad, grad_up, grad_down, vector_grad), "dp"
    )
    mix_all = mix_all / live_total
    up_all = up_all / live_total
    down_all = down_all / live_total
    vector_all = vector_all / live_total
    square_sum = (
        jnp.sum(mix_all * mix_all)
        + jnp.sum(up_all * up_all)
        + jnp.sum(down_all * down_all)
        + jnp.sum(vector_all * vector_all)
    )
    mix_part = lax.dynamic_slice_in_dim(mix_all, rank * shard_width, shard_width, 1)
    up_part = lax.dynamic_slice_in_dim(up_all, rank * shard_width, shard_width, 0)
    down_part = lax.dynamic_slice_in_dim(down_all, rank * shard_hidden, shard_hidden, 0)
    vector_part = lax.dynamic_slice_in_dim(vector_all, rank * shard_width, shard_width, 1)
    grad_norm = jnp.sqrt(square_sum)
    clip_limit = 0.03 * math.sqrt(NPARAM / (groups * FRAMES_DEV))
    clip_factor = clip_limit / jnp.maximum(grad_norm, clip_limit)
    mix_new = adamw(mix_part * clip_factor, mix_weight, mix_first, mix_second, mix_average, 0.05)
    up_new = adamw(up_part * clip_factor, up_weight, up_first, up_second, up_average, 0.05)
    down_new = adamw(
        down_part * clip_factor, down_weight, down_first, down_second, down_average, 0.05
    )
    vector_new = adamw(
        vector_part * clip_factor, vector_weight, vector_first, vector_second, vector_average, 0.25
    )
    clipped_bias_grad = vector_part[12] * clip_factor
    return (
        block_output,
        input_grad,
        grad_norm,
        mix_new[0],
        mix_new[1],
        mix_new[2],
        mix_new[3],
        up_new[0],
        up_new[1],
        up_new[2],
        up_new[3],
        down_new[0],
        down_new[1],
        down_new[2],
        down_new[3],
        vector_new[0],
        vector_new[1],
        vector_new[2],
        vector_new[3],
        clipped_bias_grad,
    )


def solution(mesh):
    in_specs = (
        P("dp", None),
        P("dp", None),
        P(),
        P(None, "dp", None),
        P(None, "dp", None),
        P(None, "dp", None),
        P(None, "dp", None),
        P("dp", None),
        P("dp", None),
        P("dp", None),
        P("dp", None),
        P("dp", None),
        P("dp", None),
        P("dp", None),
        P("dp", None),
        P(None, "dp"),
        P(None, "dp"),
        P(None, "dp"),
        P(None, "dp"),
    )
    out_specs = (
        P("dp", None),
        P("dp", None),
        P(),
        P(None, "dp", None),
        P(None, "dp", None),
        P(None, "dp", None),
        P(None, "dp", None),
        P("dp", None),
        P("dp", None),
        P("dp", None),
        P("dp", None),
        P("dp", None),
        P("dp", None),
        P("dp", None),
        P("dp", None),
        P(None, "dp"),
        P(None, "dp"),
        P(None, "dp"),
        P(None, "dp"),
        P("dp"),
    )
    return jax.shard_map(body, mesh=mesh, in_specs=in_specs, out_specs=out_specs, check_vma=False)
```

profile of v0, /device:TPU:0, one launch (start us, length us, event | category | flops | bytes accessed | tf_op | source)
XLA Modules:
  0.0 800.0 jit_solution(14471387906897489941)
XLA Ops:
  12.8 43.6 %all_gather.12 = bf16[28,512]{0,1:T(8,128)(2,1)S(1)} all-gather(bf16[28,16]{0,1:T(8,128)(2,1)S(1)} %convert_element_type.166), channel_id=1, replica_groups=mesh['dp'=32] {'dp'}, dimensions={1}, use_global_device_ids=true | all-gather | bytes 29568 | tf_op jit(solution)/shard_map/all_gather | solution.py:95
  127.4 53.7 %while.32 = (s32[]{:T(128)}, bf16[4,512,4,128]{1,3,2,0:T(8,128)(2,1)}, f32[4,4,512,1]{2,1,3,0:T(4,128)}, s32[4]{0:T(128)S(1)}, bf16[2066,4,128]{2,0,1:T(8,128)(2...) while((s32[]{:T(128)}, ...), condition=%wide.region_13.14_spmd.clone, body=%wide.region_10.13_spmd.clone.sunk | while | flops 569582592 | bytes 36957740 | solution.py:167
  193.3 46.6 %multiply_convert_fusion.1 = (bf16[2048,2048]{1,0:T(8,128)(2,1)}, f32[2048,2048]{1,0:T(8,128)}, f32[2048,2048]{1,0:T(8,128)}) fusion(f32[2048]{0:T(1024)S(1)} %bitcast.186, bf16[512,2048]{1,0:T(8,128)(2,1)} %all-gather.6.cloned.1.call-done, f32[2048,512]{0,1:T(8,128)} %copy-done.9, f32[512]{0:T(512)S(1)} %get-tuple-element.562, ...), kind=kOutput, calls=%fused_computation.64 | convolution fusion | flops 4577034240 | bytes 48263168 | tf_op jit(solution)/shard_map/dot_general | solution.py:173
  240.0 19.1 %convert_reduce_fusion = (f32[2048]{0:T(1024)}, bf16[2048,2048]{1,0:T(8,128)(2,1)}) fusion(f32[2048,2048]{1,0:T(8,128)} %get-tuple-element.660, bf16[2048,512]{0,1:T(8,128)(2,1)S(1)} %copy-done.23, bf16[2048,512]{1,0:T(8,128)(2,1)} %all-gather.8.cloned.1.call-done, f32[2048,2048]{1,0:T(8,128)} %get-tuple-element.695, f32[2048]{0:T(1024)S(1)} %bitcast.187), kind=kOutput, calls=%fused_computation.62 | convolution fusion | flops 4366268416 | bytes 46153728 | tf_op jit(solution)/shard_map/fj,ij->fi/dot_general | solution.py:184
  259.0 11.3 %fusion.110 = f32[512,2048]{1,0:T(8,128)} fusion(bf16[2048,2048]{1,0:T(8,128)(2,1)} %get-tuple-element.703, f32[2048,512]{0,1:T(8,128)} %copy-done.9, f32[512]{0:T(512)S(1)} %get-tuple-element.562, f32[512]{0:T(512)S(1)} %get-tuple-element.563, f32[2048]{0:T(1024)S(1)} %add_rsqrt_fusion, f32[2048]{0:T(1024)S(1)} %broadcast_multiply_fusion.10), kind=kOutput, calls=%fused_computation.280 | convolution fusion | flops 4300210176 | bytes 16797696 | tf_op jit(solution)/shard_map/fi,fj->ij/dot_general | solution.py:44
  270.3 7.1 fusion.126
  288.2 10.2 %fusion.127 = f32[2048,512]{1,0:T(8,128)} fusion(bf16[2048,2048]{1,0:T(8,128)(2,1)} %get-tuple-element.659, bf16[2048,512]{0,1:T(8,128)(2,1)S(1)} %copy-done.23), kind=kOutput, calls=%fused_computation.289 | convolution fusion | flops 4294967296 | bytes 14680064 | tf_op jit(solution)/shard_map/fi,fj->ij/dot_general | solution.py:44
  298.5 17.1 %multiply_reduce_fusion.10 = (f32[512]{0:T(512)}, f32[512]{0:T(512)}, f32[2048,512]{0,1:T(8,128)}, bf16[2048,512]{0,1:T(8,128)(2,1)S(1)}) fusion(f32[2048,512]{0,1:T(8,128)} %copy.191, f32[512]{0:T(512)S(1)} %copy-done.113, f32[2048]{0:T(1024)S(1)} %copy-done.29, f32[2048,512]{0,1:T(8,128)} %get-tuple-element.694, f32[512]{0:T(512)S(1)} %copy-done.98, ...), kind=kOutput, calls=%fused_computation.121 | convolution fusion | flops 4315937792 | bytes 33607680 | tf_op jit(solution)/shard_map/dot_general | solution.py:178
  333.7 157.8 %while.33 = (s32[]{:T(128)}, f32[2066,4,128]{2,0,1:T(8,128)}, f32[2066,4,128]{2,0,1:T(8,128)}, bf16[4,512,4,128]{1,3,2,0:T(8,128)(2,1)}, s32[4]{0:T(128)S(1)}, /...) while((s32[]{:T(128)}, f32[2066,4,128]{2,0,1:T(8,128)}, ...), condition=%wide.region_20.21_spmd.clone, body=%wide.region_18.20_spmd.clone.sunk | while | flops 1408084992 | bytes 65920632 | solution.py:234
  353.4 6.2 dynamic_update_slice.48
  364.8 6.2 dynamic_update_slice.49
  393.1 6.2 dynamic_update_slice.48
  404.5 6.2 dynamic_update_slice.49
  432.7 6.2 dynamic_update_slice.48
  444.2 6.2 dynamic_update_slice.49
  472.3 5.7 dynamic_update_slice.48
  483.3 5.7 dynamic_update_slice.49
  541.0 8.5 %multiply_multiply_fusion.10 = (f32[2048,512]{0,1:T(8,128)S(1)}, f32[2048,512]{0,1:T(8,128)S(1)}) fusion(f32[2048,512]{0,1:T(8,128)} %get-tuple-element.696, f32[2048,512]{0,1:T(8,128)} %copy-done.10, f32[2048]{0:T(1024)S(1)} %broadcast_multiply_fusion.4, f32[2048]{0:T(1024)S(1)} %broadcast_multiply_fusion.5, f32[512]{0:T(512)S(1)} %copy-done.93, ...), kind=kLoop, calls=%fused_computation.137 | loop fusion | flops 16777216 | bytes 25243648 | tf_op jit(solution)/shard_map/mul | solution.py:259
  557.6 7.7 slice_multiply_fusion.1
  565.4 16.3 %multiply_reduce_fusion.3 = (f32[512]{0:T(512)S(1)}, f32[512]{0:T(512)S(1)}, f32[512]{0:T(512)S(1)}, f32[512]{0:T(512)S(1)}, f32[512]{0:T(512)S(1)}, /*index=5*/...) fusion(f32[2048,512]{0,1:T(8,128)S(1)} %multiply_multiply_fusio, ...), kind=kLoop, calls=%fused_computation.114 | loop fusion | flops 51370496 | bytes 52494336 | tf_op jit(solution)/shard_map/reduce_sum | solution.py:262
  581.8 5.9 fusion.71
  594.0 40.4 %psum.31 = f32[28,512]{0,1:T(8,128)S(1)} all-reduce(f32[28,512]{0,1:T(8,128)S(1)} %copy.205), channel_id=1, replica_groups=mesh['dp'=32] {'dp'}, use_global_device_ids=true, to_apply=%region_61.62 | all-reduce | flops 14336 | bytes 114688 | tf_op jit(solution)/shard_map/psum | solution.py:312
  635.1 134.4 %all-reduce.14.cloned.1.call-done = (f32[4,512,512]{2,1,0:T(8,128)}, f32[512,2048]{1,0:T(8,128)}, f32[2048,512]{1,0:T(8,128)}) async-done(((f32[4,512,512]{2,1,0:T(8,128)}, f32[512,2048]{1,0:T(8,128)}, f32[2048,512]{1,0:T(8,128)}), (f32[4,512,512]{2,1,0:T(8,128)}, f32[512,2048]{1,0:T(8,128)}, f32[2048,512]{1,0:T(8,128)})) %all-reduce.14.cloned.1.call-update) | async-done | bytes 12582928 | tf_op jit(solution)/shard_map/psum | solution.py:312
  769.5 6.0 multiply_reduce_fusion.18
  (465 shorter events, 320.7 us)
Async XLA Ops:
  7.2 52.8 %copy-start.107 = (s32[32,2]{0,1:T(2,128)S(1)}, s32[32,2]{0,1:T(2,128)}, u32[]{:S(2)}) copy-start(s32[32,2]{0,1:T(2,128)} %param.25) | copy-start | bytes 772
  7.2 86.3 %all-gather.4.cloned.1.call-start = ((), (), s32[]{:S(2)}) async-start(), calls=%async_computation | async-start | bytes 2162688 | tf_op jit(solution)/shard_map/all_gather | solution.py:92
  8.8 184.5 %all-gather.6.cloned.1.call-start = ((), (), s32[]{:S(2)}) async-start(), calls=%async_computation.1 | async-start | bytes 2162688 | tf_op jit(solution)/shard_map/all_gather | solution.py:93
  10.4 229.5 %all-gather.8.cloned.1.call-start = ((), (), s32[]{:S(2)}) async-start(), calls=%async_computation.2 | async-start | bytes 2162688 | tf_op jit(solution)/shard_map/all_gather | solution.py:94
  12.1 757.4 %all-reduce.14.cloned.1.call-start = ((), (), s32[]{:S(2)}) async-start(), calls=%async_computation.3 | async-start | bytes 25165824 | tf_op jit(solution)/shard_map/psum | solution.py:312
  59.1 20.8 %copy-start.71 = (f32[512]{0:T(512)}, f32[512]{0:T(512)S(1)}, u32[]{:S(2)}) copy-start(f32[512]{0:T(512)S(1)} %get-tuple-element.567) | copy-start | bytes 6148
  59.1 20.8 %copy-start.73 = (f32[512]{0:T(512)}, f32[512]{0:T(512)S(1)}, u32[]{:S(2)}) copy-start(f32[512]{0:T(512)S(1)} %get-tuple-element.573) | copy-start | bytes 6148
  59.1 20.8 %copy-start.77 = (f32[512]{0:T(512)}, f32[512]{0:T(512)S(1)}, u32[]{:S(2)}) copy-start(f32[512]{0:T(512)S(1)} %get-tuple-element.566) | copy-start | bytes 6148
  59.2 20.8 %copy-start.79 = (f32[512]{0:T(512)}, f32[512]{0:T(512)S(1)}, u32[]{:S(2)}) copy-start(f32[512]{0:T(512)S(1)} %get-tuple-element.568) | copy-start | bytes 6148
  59.2 20.8 %copy-start.85 = (f32[512]{0:T(512)}, f32[512]{0:T(512)S(1)}, u32[]{:S(2)}) copy-start(f32[512]{0:T(512)S(1)} %get-tuple-element.572) | copy-start | bytes 6148
  59.2 20.8 %copy-start.87 = (f32[512]{0:T(512)}, f32[512]{0:T(512)S(1)}, u32[]{:S(2)}) copy-start(f32[512]{0:T(512)S(1)} %get-tuple-element.574) | copy-start | bytes 6148
  59.2 30.0 %copy-start.69 = (f32[512]{0:T(512)}, f32[512]{0:T(512)S(1)}, u32[]{:S(2)}) copy-start(f32[512]{0:T(512)S(1)} %get-tuple-element.577) | copy-start | bytes 6148
  59.2 43.0 %copy-start.99 = (f32[512]{0:T(512)}, f32[512]{0:T(512)S(1)}, u32[]{:S(2)}) copy-start(f32[512]{0:T(512)S(1)} %get-tuple-element.571) | copy-start | bytes 6148
  59.2 43.0 %copy-start.108 = (f32[512]{0:T(512)}, f32[512]{0:T(512)S(1)}, u32[]{:S(2)}) copy-start(f32[512]{0:T(512)S(1)} %get-tuple-element.570) | copy-start | bytes 6148
  59.2 52.1 %copy-start.92 = (f32[512]{0:T(512)}, f32[512]{0:T(512)S(1)}, u32[]{:S(2)}) copy-start(f32[512]{0:T(512)S(1)} %get-tuple-element.565) | copy-start | bytes 6148
  59.2 126.1 %copy-start.97 = (f32[512]{0:T(512)}, f32[512]{0:T(512)S(1)}, u32[]{:S(2)}) copy-start(f32[512]{0:T(512)S(1)} %get-tuple-element.564) | copy-start | bytes 6148
  60.0 20.0 %copy-start.60 = (f32[512]{0:T(512)}, f32[512]{0:T(512)S(1)}, u32[]{:S(2)}) copy-start(f32[512]{0:T(512)S(1)} %get-tuple-element.582) | copy-start | bytes 6148
  60.0 20.0 %copy-start.62 = (f32[512]{0:T(512)}, f32[512]{0:T(512)S(1)}, u32[]{:S(2)}) copy-start(f32[512]{0:T(512)S(1)} %get-tuple-element.581) | copy-start | bytes 6148
  60.0 125.3 %copy-start.89 = (f32[512]{0:T(512)}, f32[512]{0:T(512)S(1)}, u32[]{:S(2)}) copy-start(f32[512]{0:T(512)S(1)} %get-tuple-element.579) | copy-start | bytes 6148
  60.5 124.8 %copy-start.28 = (f32[2048]{0:T(1024)}, f32[2048]{0:T(1024)S(1)}, u32[]{:S(2)}) copy-start(f32[2048]{0:T(1024)S(1)} %compare_convert_fusion.1) | copy-start | bytes 24580
  69.9 115.4 %copy-start = (bf16[2048,512]{0,1:T(8,128)(2,1)}, bf16[2048,512]{0,1:T(8,128)(2,1)S(1)}, u32[]{:S(2)}) copy-start(bf16[2048,512]{0,1:T(8,128)(2,1)S(1)} %copy.181) | copy-start | bytes 6291460
  85.2 26.1 %copy-start.58 = (f32[2048]{0:T(1024)}, f32[2048]{0:T(1024)S(1)}, u32[]{:S(2)}) copy-start(f32[2048]{0:T(1024)S(1)} %broadcast_multiply_fusion.11) | copy-start | bytes 24580
  87.8 23.5 %copy-start.66 = (f32[2048]{0:T(1024)}, f32[2048]{0:T(1024)S(1)}, u32[]{:S(2)}) copy-start(f32[2048]{0:T(1024)S(1)} %add_rsqrt_fusion.1) | copy-start | bytes 24580
  193.3 46.6 %copy-start.23 = (bf16[2048,512]{0,1:T(8,128)(2,1)S(1)}, bf16[2048,512]{0,1:T(8,128)(2,1)}, u32[]{:S(2)}) copy-start(bf16[2048,512]{0,1:T(8,128)(2,1)} %get-tuple-element.647) | copy-start | bytes 6291460
  (115 other events, 745.8 us)
Sparse Core Ops, SparseCore 0:
  11.5 58.7 all-gather.3
  73.8 55.3 all-gather.5
  132.6 55.2 all-gather.7
  541.1 228.3 all-reduce.13
where the time goes:
time: 807 us; the launch traced here: 800 us
  matrix products  257 us (32%)
  local copies, waits for them, and re-layouts  144 us (18%)
  waiting for transfers between devices  135 us (17%)
  other arithmetic  123 us (15%)
  blocking collectives  83.9 us (10%)
  loops' own time  36.9 us (5%)
  between operations  19.9 us (2%)
    psum x1, waiting for transfers between devices, body(): lax.psum((mix_grad, grad_up, grad_down, vector_grad), 'dp')  134 us
    dot_general x1, matrix products, body(): jnp.dot(normed_low, up_full, preferred_element_type=jnp.float32)  46.6 us
    all_gather x1, blocking collectives, body(): lax.all_gather(vector_weight.astype(jnp.bfloat16), 'dp', axis=1, tiled=True)  43.6 us
    psum x1, blocking collectives, body(): lax.psum((mix_grad, grad_up, grad_down, vector_grad), 'dp')  40.4 us
    dot_general x6, matrix products, contract(): jnp.einsum('fi,fj->ij', left, right, preferred_element_type=jnp.float32)  31.7 us
    unnamed x236, local copies, waits for them, and re-layouts  27.4 us
    dot_general x8, matrix products, scores_of(): jnp.einsum('qhe,khe->hqk', query_rows, key_rows, preferred_element_type=j...  25.3 us
    dynamic_update_slice x4, local copies, waits for them, and re-layouts, attend_back(): lax.dynamic_update_slice_in_dim(value_acc, lax.dynamic_slice_in_dim(value...  24.3 us
  transfers between devices with their start and end apart: 4, of which 1 were waited for; matrix products, arithmetic and copies ran while one was open for 26% of the time, Pallas kernels for 0%

commit v1 on v0

v1 whole, which is shorter than its diff:
```python
import functools
import math

import jax
import jax.numpy as jnp
from jax import lax
from jax.experimental import pallas as pl
from jax.experimental.pallas import tpu as pltpu
from jax.sharding import PartitionSpec as P

HEADS = 4
HEAD = 128
WINDOW = 19
RADIUS = WINDOW // 2
STEP = 10
FRAMES_DEV = 2048
NPARAM = 3160064
D = 512
FF = 2048
ROWS = 256
SUB = 32
PAIR = 128
MID_ROWS = 512
TALL = 64
CHUNK = 256
TILE = 96
HALO = 16
SPAN = TILE + 2 * HALO
FACTOR = HEAD**-0.5
LOG2_E = math.log2(math.e)
F32 = jnp.float32
BF16 = jnp.bfloat16
ANY = pl.BlockSpec(memory_space=pl.ANY)
IN_VMEM = pl.BlockSpec(memory_space=pltpu.VMEM)
IN_SMEM = pl.BlockSpec(memory_space=pltpu.SMEM)
VMEM_LIMIT = 62 * 1024 * 1024


def mm(left, right):
    return jnp.dot(left, right, preferred_element_type=F32)


def mm_nt(left, right):
    return lax.dot_general(left, right, (((1,), (1,)), ((), ())), preferred_element_type=F32)


def normalise(value):
    center = value - jnp.mean(value, axis=-1, keepdims=True)
    scale = lax.rsqrt(jnp.mean(center * center, axis=-1, keepdims=True) + 1e-05)
    return center * scale, scale


def norm_back(upstream, gain, normal, scale):
    inner = upstream * gain
    along = jnp.mean(inner * normal, axis=-1, keepdims=True)
    return scale * (inner - jnp.mean(inner, axis=-1, keepdims=True) - normal * along)


def total(value):
    return jnp.sum(value, axis=0, keepdims=True)


def video_ends(len_ref):
    rank = lax.axis_index("dp")
    first = len_ref[0, rank]
    return first, first + len_ref[1, rank]


def wide(column):
    return jnp.concatenate([column] * (D // 128), axis=1)


def row_index(start):
    return start + lax.broadcasted_iota(jnp.int32, (SUB, 128), 0)


def live_rows(start, ends):
    return wide((row_index(start) < ends[1]).astype(F32))


def copy_all(pairs, sems):
    copies = [pltpu.make_async_copy(src, dst, sems.at[i]) for i, (src, dst) in enumerate(pairs)]
    for copy in copies:
        copy.start()
    return copies


def attention_mask(start, ends, frames):
    t = start + lax.broadcasted_iota(jnp.int32, (TILE, SPAN), 0)
    u = start - HALO + lax.broadcasted_iota(jnp.int32, (1, SPAN), 1)
    one, none = jnp.int32(64), jnp.int32(0)

    def code(spot):
        return (
            spot
            + jnp.where(spot >= ends[0], one, none)
            + jnp.where(spot >= ends[1], one, none)
            + jnp.where(spot >= frames, one, none)
        )

    return jnp.abs(code(t) - (code(u) + jnp.where(u < 0, -one, none))) <= RADIUS


def inside(spot, ends, frames):
    first = (spot == 0) | (spot == ends[0]) | (spot == ends[1])
    last = (spot == frames - 1) | (spot == ends[0] - 1) | (spot == ends[1] - 1)
    return wide(1.0 - first.astype(F32)), wide(1.0 - last.astype(F32))


def shifted(window, size, spot, ends, frames):
    not_first, not_last = inside(spot, ends, frames)
    return window[7 : size + 7] * not_first, window[8 : size + 8], window[9 : size + 9] * not_last


def slot_of(owner):
    z, y, x, core = owner // 8, owner // 4 % 2, owner // 2 % 2, owner % 2
    return ((core * 2 + y) * 2 + x) * 4 + z


def whole_matrix(slots, rows, cols=slice(None)):
    return jnp.concatenate([slots[slot_of(owner), rows, cols] for owner in range(D // WIDTH)], axis=0)


def early_matrix(early, j):
    return whole_matrix(early, slice(j * WIDTH, (j + 1) * WIDTH))


def front_kernel(near, len_ref, x_in, *refs):
    if near:
        mix_ref, up_ref, down_ref, wvec_ref, vec_ref, up_out, down_out, *refs = refs
    else:
        early, vec_ref, *refs = refs
    outs, refs = refs[:8], refs[8:]
    kept, refs = refs[:8], refs[8:]
    xh, x3, rs, n3t, qkv, wt, p, o = kept
    x, low, sems, *refs = refs
    q, kp, vp = (qkv.at[j] for j in range(3))
    frames = x.shape[0]
    tiles = p.shape[0] // TILE
    steps = frames // ROWS
    ends = video_ends(len_ref)
    load = pltpu.make_async_copy(x_in, x, sems.at[8])
    load.start()
    if near:
        early, up_slots, down_slots, tables, *refs = refs
        z, y, x_, core = place()
        me = ((core * 2 + y) * 2 + x_) * 4 + z
        greet()
        tables[me, :, 0 : wvec_ref.shape[1]] = wvec_ref[...].astype(BF16)
        first = Gather(tables, refs[0])
        first.start_z()
        for j in range(3):
            early[me, j * WIDTH : (j + 1) * WIDTH, :] = mix_ref[j].astype(BF16)
        second = Gather(early, refs[1])
        second.start_z()
        up_slots[me, 0:WIDTH, :] = mix_ref[3].astype(BF16)
        for c in range(FF // D):
            up_slots[me, (c + 1) * WIDTH : (c + 2) * WIDTH, :] = up_ref[:, c * D : (c + 1) * D].astype(BF16)
        third = Gather(up_slots, refs[2])
        third.start_z()
        down_slots[me] = down_ref[...].astype(BF16)
        fourth = Gather(down_slots, refs[3])
        fourth.start_z()
    zero8 = jnp.zeros((8, D), F32)
    xh[0:8, :] = zero8
    xh[frames + 8 : frames + 16, :] = zero8
    q[frames:, :] = jnp.zeros((q.shape[0] - frames, D), BF16)
    for ref in (kp, vp):
        ref[0:HALO, :] = jnp.zeros((HALO, D), BF16)
        ref[frames + HALO :, :] = jnp.zeros((ref.shape[0] - frames - HALO, D), BF16)
    load.wait()

    def norm_step(i, carry):
        for s in range(PAIR // SUB):
            start = pl.multiple_of(i * PAIR + s * SUB, SUB)
            normal, scale = normalise(x[pl.ds(start, SUB), :].astype(F32))
            xh[pl.ds(start + 8, SUB), :] = normal
            rs[pl.ds(start, SUB), :] = jnp.broadcast_to(scale, (SUB, 128))
        return carry

    lax.fori_loop(0, frames // PAIR, norm_step, 0)
    copies = [pltpu.make_async_copy(kept[i], outs[i], sems.at[i]) for i in range(6)]
    copies[0].start()
    if near:
        first.all_along_z()
        first.all_arrive()
        second.along_z()
        table = whole_matrix(tables, slice(None))
    else:
        table = whole_matrix(early, slice(3 * WIDTH, None), slice(0, 128))
    table = table.astype(F32).T
    vec_ref[...] = table[0 : vec_ref.shape[0]]

    marks = (frames // PAIR * 3 // 8, frames // PAIR * 3 // 4)

    def conv_step(i, carry):
        if near:

            @pl.when(i == marks[0])
            def _():
                second.in_plane()

            @pl.when(i == marks[1])
            def _():
                second.diagonal()

        for s in range(PAIR // SUB):
            start = pl.multiple_of(i * PAIR + s * SUB, SUB)
            rows = pl.ds(start, SUB)
            live = live_rows(start, ends)
            window = xh[pl.ds(start, SUB + 16), :] * vec_ref[0:1, :] + vec_ref[1:2, :]
            before, own, after = shifted(window, SUB, row_index(start), ends, frames)
            scales = []
            for j, (gain, shift, taps) in enumerate(((2, 3, 15), (4, None, 18), (5, 6, 21))):
                conv = live * (
                    vec_ref[taps : taps + 1, :] * before
                    + vec_ref[taps + 1 : taps + 2, :] * own
                    + vec_ref[taps + 2 : taps + 3, :] * after
                )
                normal, scale = normalise(conv)
                scales.append(scale)
                x3[j, rows, :] = normal
                normed = normal * vec_ref[gain : gain + 1, :]
                if shift is not None:
                    normed = normed + vec_ref[shift : shift + 1, :]
                low[j, rows, :] = normed.astype(BF16)
            lane = lax.broadcasted_iota(jnp.int32, (SUB, 128), 1)
            scale = rs[rows, :]
            for j in range(3):
                scale = jnp.where(lane == j, scales[j], scale)
            rs[rows, :] = scale
        return carry

    def project_step(i, carry):
        top = pl.multiple_of(i * ROWS, ROWS)
        rows = pl.ds(top, ROWS)
        padded = pl.ds(top + HALO, ROWS)
        nq, nk, nv = (low[j, rows, :] for j in range(3))
        q[rows, :] = ((mm(nq, early_matrix(early, 0)) + vec_ref[9:10, :]) * FACTOR).astype(BF16)
        kp[padded, :] = mm(nk, early_matrix(early, 1)).astype(BF16)
        vp[padded, :] = (mm(nv, early_matrix(early, 2)) + vec_ref[10:11, :]).astype(BF16)
        n3t[0, :, rows] = nq.T
        n3t[1, :, rows] = nk.T
        n3t[2, :, rows] = nv.T
        return carry

    lax.fori_loop(0, frames // PAIR, conv_step, 0)
    for i in (1, 2):
        copies[i].start()
    if near:
        third.along_z()
        second.arrive()
    lax.fori_loop(0, steps, project_step, 0)
    if near:
        fourth.along_z()
    for j in range(3):
        wt[j] = early_matrix(early, j).T
    for i in (3, 4, 5):
        copies[i].start()

    def attend(start):
        allowed = attention_mask(start, ends, frames)
        heads = [slice(head * HEAD, (head + 1) * HEAD) for head in range(HEADS)]
        scores = [mm_nt(q[pl.ds(start, TILE), cols], kp[pl.ds(start, SPAN), cols]) for cols in heads]
        masked = [jnp.where(allowed, score, -1e30) for score in scores]
        tops = [jnp.max(score, axis=-1, keepdims=True) for score in masked]
        weights = [jnp.exp2((score - top) * LOG2_E) for score, top in zip(masked, tops)]
        sums = [jnp.sum(weight, axis=-1, keepdims=True) for weight in weights]
        probs = [weight * pltpu.reciprocal(count, approx=True) for weight, count in zip(weights, sums)]
        for prob, cols in zip(probs, heads):
            p[pl.ds(start, TILE), cols] = prob
        mixed = [mm(prob.astype(BF16), vp[pl.ds(start, SPAN), cols]) for prob, cols in zip(probs, heads)]
        for value, cols in zip(mixed, heads):
            o[pl.ds(start, TILE), cols] = value.astype(BF16)

    pairs = tiles // 2
    most = pairs * 3 // 4
    leaving = [
        pltpu.make_async_copy(kept[j].at[rows], outs[j].at[rows], sems.at[9 + 2 * k + j - 6])
        for k, rows in enumerate((pl.ds(0, most * 2 * TILE), pl.ds(most * 2 * TILE, (pairs - most) * 2 * TILE)))
        for j in (6, 7)
    ]

    def attend_step(i, carry):
        if near:

            @pl.when(i == pairs // 4)
            def _():
                third.in_plane()

            @pl.when(i == pairs // 2)
            def _():
                third.diagonal()
                fourth.in_plane()

            @pl.when(i == pairs - 2)
            def _():
                fourth.diagonal()

        @pl.when(i == most)
        def _():
            for copy in leaving[:2]:
                copy.start()

        for k in range(2):
            attend(pl.multiple_of((2 * i + k) * TILE, 32))
        return carry

    lax.fori_loop(0, pairs, attend_step, 0)
    parts = leaving
    for copy in leaving[2:]:
        copy.start()
    if near:
        third.arrive()
        up_copy = pltpu.make_async_copy(up_slots, up_out, sems.at[13])
        up_copy.start()
        fourth.arrive()
        down_copy = pltpu.make_async_copy(down_slots, down_out, sems.at[14])
        down_copy.start()
        for part in (first, second, third, fourth):
            part.sent_all()
        parts = parts + [up_copy, down_copy]
    for copy in copies + parts:
        copy.wait()


def front(near, lengths, x, weights):
    frames = x.shape[0]
    tiles = -(-frames // TILE)
    padded = tiles * TILE
    spread = (tiles - 1) * TILE + SPAN
    owners = D // WIDTH
    dma = pltpu.SemaphoreType.DMA
    shapes = [
        ((frames + 16, D), F32),
        ((3, frames, D), F32),
        ((frames, 128), F32),
        ((3, D, frames), BF16),
        ((3, spread, D), BF16),
        ((3, D, D), BF16),
        ((padded, D), F32),
        ((padded, D), BF16),
    ]
    outs = [((32, D), F32)]
    scratch = shapes + [((frames, D), BF16), ((3, frames, D), BF16)]
    scratch = [pltpu.VMEM(shape, kind) for shape, kind in scratch] + [dma((15,))]
    params = dict(vmem_limit_bytes=VMEM_LIMIT)
    if near:
        outs += [((owners, UP, D), BF16), ((owners, DOWN, D), BF16)]
        scratch += [pltpu.VMEM((owners, *slot), BF16) for slot in ((3 * WIDTH, D), (UP, D), (DOWN, D), (WIDTH, 128))]
        scratch += [dma((6,))] * 4
        params.update(collective_id=0, has_side_effects=True)
    return pl.pallas_call(
        functools.partial(front_kernel, near),
        out_shape=[jax.ShapeDtypeStruct(shape, kind) for shape, kind in outs + shapes],
        in_specs=[IN_SMEM, ANY] + [IN_VMEM] * len(weights),
        out_specs=[IN_VMEM] + [ANY] * (len(outs) - 1 + len(shapes)),
        scratch_shapes=scratch,
        compiler_params=pltpu.CompilerParams(**params),
        name="front",
    )(lengths, x, *weights)


def gelu_pair(z):
    phi = lax.erf(z * math.sqrt(0.5)) * 0.5 + 0.5
    bell = jnp.exp2(z * z * (-0.5 * LOG2_E))
    return z * phi, phi + z * bell * (1.0 / math.sqrt(2.0 * math.pi))


def fold(value):
    return jnp.sum(value.reshape(value.shape[0] // 8, 8, value.shape[1]), axis=0)


def deal(sums, rows, value, first=0):
    size = rows.stop - rows.start
    for k in range(value.shape[0] // size):
        slot = slot_of(first + k)
        sums[slot // 16, slot % 16, rows, :] = value[k * size : (k + 1) * size].astype(sums.dtype)


def middle_kernel(
    len_ref, o_in, x_in, dy_in, vec_ref, up_in, down_in,
    out_out, dx_out, do_out, up_out, down_out, gvec,
    o, x, dy, out, up_sums, down_sums, slots, down_slots, gel, dz1, n2t, dz2t, ot, da, keep_pj, keep_mid, keep_xh, keep_r,
    acc, in_sems, row_sems, out_sems,
):
    frames = x.shape[0]
    steps = frames // MID_ROWS
    ends = video_ends(len_ref)
    load_slots = [
        pltpu.make_async_copy(src, dst, in_sems.at[i]) for i, (src, dst) in enumerate(((up_in, slots), (down_in, down_slots)))
    ]
    cut = MID_ROWS
    row_loads = [
        [
            pltpu.make_async_copy(src.at[rows], dst.at[rows], row_sems.at[k, half])
            for k, (src, dst) in enumerate(((o_in, o), (x_in, x), (dy_in, dy)))
        ]
        for half, rows in enumerate((pl.ds(0, cut), pl.ds(cut, frames - cut)))
    ]
    for load in [row_loads[0][0], *load_slots, *row_loads[0][1:], *row_loads[1]]:
        load.start()
    acc[...] = jnp.zeros_like(acc)
    for load in load_slots + row_loads[0]:
        load.wait()

    def add(row, value):
        acc[row] += fold(value)

    def up_rows(c):
        return slice((c + 1) * WIDTH, (c + 2) * WIDTH)

    def down_rows(start, size):
        each = 4 * WIDTH
        return jnp.concatenate([down_slots[slot_of(k)] for k in range(start // each, (start + size) // each)], axis=0)

    def step(i, carry):
        top = pl.multiple_of(i * MID_ROWS, MID_ROWS)
        all_rows = pl.ds(top, MID_ROWS)

        @pl.when(i == 1)
        def _():
            for load in row_loads[1]:
                load.wait()

        s1, s2 = vec_ref[13:14, :], vec_ref[14:15, :]
        ot[:, all_rows] = o[all_rows, :].T
        n2, dz2 = [None, None], [None, None]

        def half_rows(h):
            return pl.ds(pl.multiple_of(top + h * ROWS, ROWS), ROWS)

        def project(h):
            return mm(o[half_rows(h), :], whole_matrix(slots, slice(0, WIDTH)))

        def norm_half(h, projected):
            low_n2, low_dz2 = [], []
            for s in range(ROWS // SUB):
                start = pl.multiple_of(top + h * ROWS + s * SUB, SUB)
                rows, here = pl.ds(start, SUB), slice(h * ROWS + s * SUB, h * ROWS + (s + 1) * SUB)
                live = live_rows(start, ends)
                value = projected[s * SUB : (s + 1) * SUB] + vec_ref[11:12, :]
                keep_pj[here, :] = value
                mid = live * (x[rows, :].astype(F32) + s1 * value)
                keep_mid[here, :] = mid
                normal, scale = normalise(mid)
                keep_xh[here, :] = normal
                keep_r[here, :] = jnp.broadcast_to(scale, (SUB, 128))
                low_n2.append((normal * vec_ref[7:8, :] + vec_ref[8:9, :]).astype(BF16))
                low = (s2 * (live * dy[rows, :])).astype(BF16)
                add(4, low.astype(F32))
                low_dz2.append(low)
            n2[h], dz2[h] = jnp.concatenate(low_n2, axis=0), jnp.concatenate(low_dz2, axis=0)

        def back_blocks(h, z2, dn2, blocks):
            for s in blocks:
                start = pl.multiple_of(top + h * ROWS + s * SUB, SUB)
                rows, here = pl.ds(start, SUB), slice(h * ROWS + s * SUB, h * ROWS + (s + 1) * SUB)
                spot = slice(s * SUB, (s + 1) * SUB)
                live = live_rows(start, ends)
                z2_live = live * (z2[spot] + vec_ref[12:13, :])
                out[rows, :] = (keep_mid[here, :] + s2 * z2_live).astype(BF16)
                dy_rows = dy[rows, :]
                add(5, dy_rows * z2_live)
                normal = keep_xh[here, :]
                up = dn2[spot]
                add(0, up * normal)
                add(1, up)
                dx1 = dy_rows + norm_back(up, vec_ref[7:8, :], normal, keep_r[here, 0:1])
                dy[rows, :] = dx1
                dx_live = dx1 * live
                add(2, dx_live * keep_pj[here, :])
                low = (s1 * dx_live).astype(BF16)
                add(3, low.astype(F32))
                da[rows, :] = low

        def back_dot(h):
            o[half_rows(h), :] = mm_nt(da[half_rows(h), :], whole_matrix(slots, slice(0, WIDTH))).astype(BF16)

        def z2_dot(h):
            return mm(gel[half_rows(h), :], down_rows(0, FF))

        def dn2_dot(h):
            return sum(
                mm_nt(dz1[half_rows(h), c * D : (c + 1) * D], whole_matrix(slots, up_rows(c))) for c in range(FF // D)
            )

        projected = [project(0), project(1)]
        norm_half(0, projected[0])

        units = [(c, h) for c in range(FF // CHUNK) for h in range(MID_ROWS // ROWS)]

        def inner(c):
            return slice(c * CHUNK % D, c * CHUNK % D + CHUNK)

        def up_dot(c, h):
            return mm(n2[h], whole_matrix(slots, up_rows(c * CHUNK // D), inner(c)))

        def down_dot(c, h):
            return mm_nt(dz2[h], down_rows(c * CHUNK, CHUNK))

        def activate(c, h, z1, dgel, blocks):
            cols = slice(c * CHUNK, (c + 1) * CHUNK)
            big = c * CHUNK // D
            for s in blocks:
                here = slice(s * TALL, (s + 1) * TALL)
                rows = pl.ds(pl.multiple_of(top + h * ROWS + s * TALL, TALL), TALL)
                value, slope = gelu_pair(z1[here] + vec_ref[24 + big : 25 + big, inner(c)])
                gel[rows, cols] = value.astype(BF16)
                back = dgel[here] * slope
                dz1[rows, cols] = back.astype(BF16)
                acc[8 + big, :, inner(c)] += fold(back)

        count = ROWS // TALL
        blocks = ROWS // SUB
        z1, dgel = up_dot(*units[0]), down_dot(*units[0])
        norm_half(1, projected[1])
        for h in range(2):
            n2t[:, half_rows(h)] = n2[h].T
            dz2t[:, half_rows(h)] = dz2[h].T
        z2 = dn2 = None
        for u, unit in enumerate(units):
            following = units[u + 1] if u + 1 < len(units) else None
            if following:
                next_z1 = up_dot(*following)
            else:
                z2 = z2_dot(0)
            activate(*unit, z1, dgel, range(count // 2))
            if following:
                next_dgel = down_dot(*following)
            else:
                dn2 = dn2_dot(0)
            activate(*unit, z1, dgel, range(count // 2, count))
            z1, dgel = next_z1, next_dgel
        next_z2 = z2_dot(1)
        back_blocks(0, z2, dn2, range(blocks // 2))
        next_dn2 = dn2_dot(1)
        back_blocks(0, z2, dn2, range(blocks // 2, blocks))
        back_dot(0)
        back_blocks(1, next_z2, next_dn2, range(blocks))
        back_dot(1)
        return carry

    lax.fori_loop(0, steps, step, 0)
    o[frames:, :] = jnp.zeros((o.shape[0] - frames, D), BF16)
    gvec[...] = jnp.sum(acc[...], axis=1)
    pairs = [(out, out_out), (dy, dx_out), (o, do_out), (up_sums, up_out), (down_sums, down_out)]
    copies = [pltpu.make_async_copy(src, dst, out_sems.at[i]) for i, (src, dst) in enumerate(pairs)]
    for copy in copies[:3]:
        copy.start()
    deal(up_sums, slice(0, WIDTH), mm(ot[...], da[...]))
    for c in range(FF // D):
        deal(up_sums, slice((c + 1) * WIDTH, (c + 2) * WIDTH), mm(n2t[...], dz1[:, c * D : (c + 1) * D]))
    copies[3].start()
    for c in range(FF // D):
        turned = mm(dz2t[...], gel[:, c * D : (c + 1) * D])
        turned = turned.astype(BF16).T if down_sums.dtype == BF16 else turned.T
        deal(down_sums, slice(0, DOWN), turned, 8 * c)
    copies[4].start()
    for copy in copies:
        copy.wait()


def middle(near, lengths, o, x, dy, vectors, up, down):
    frames = x.shape[0]
    padded = o.shape[0]
    owners = up.shape[0]
    outs = [
        ((frames, D), BF16),
        ((frames, D), F32),
        ((padded, D), BF16),
        ((2, owners // 2, UP, D), BF16 if near else F32),
        ((2, owners // 2, DOWN, D), BF16 if near else F32),
        ((16, D), F32),
    ]
    scratch = [
        ((padded, D), BF16),
        ((frames, D), BF16),
        ((frames, D), F32),
        ((frames, D), BF16),
        ((2, owners // 2, UP, D), BF16 if near else F32),
        ((2, owners // 2, DOWN, D), BF16 if near else F32),
        ((owners, UP, D), BF16),
        ((owners, DOWN, D), BF16),
        ((frames, FF), BF16),
        ((frames, FF), BF16),
        ((D, frames), BF16),
        ((D, frames), BF16),
        ((D, frames), BF16),
        ((frames, D), BF16),
        ((MID_ROWS, D), F32),
        ((MID_ROWS, D), F32),
        ((MID_ROWS, D), F32),
        ((MID_ROWS, 128), F32),
        ((16, 8, D), F32),
    ]
    return pl.pallas_call(
        middle_kernel,
        out_shape=[jax.ShapeDtypeStruct(shape, kind) for shape, kind in outs],
        in_specs=[IN_SMEM, ANY, ANY, ANY, IN_VMEM, ANY, ANY],
        out_specs=[ANY] * 5 + [IN_VMEM],
        scratch_shapes=[pltpu.VMEM(shape, kind) for shape, kind in scratch]
        + [pltpu.SemaphoreType.DMA(shape) for shape in ((2,), (3, 2), (5,))],
        compiler_params=pltpu.CompilerParams(vmem_limit_bytes=VMEM_LIMIT),
        name="middle",
    )(lengths, o, x, dy, vectors, up, down)


def back_kernel(near, len_ref, vec_ref, gmid_ref, *refs):
    if near:
        up_in, down_in, *refs = refs
    saved, refs = refs[:7], refs[7:]
    do_in, dx_in, ig_out, *refs = refs
    if near:
        early_part, up_part, down_part, vec_part, square, *refs = refs
    else:
        early_sums, gvec, *refs = refs
    rs, n3t, qkv, wt, p, xh, triple, do, refs = *refs[:8], refs[8:]
    carry_k, carry_v, acc, unit, ups, in_sems, part_sems, out_sems, *refs = refs
    q, kp, vp = (qkv.at[j] for j in range(3))
    frames = xh.shape[0] - 16
    tiles = p.shape[0] // TILE
    ends = video_ends(len_ref)
    body = pl.ds(8, frames)
    dx = p.at[0:frames]
    xh_in, x3_in, rs_in, n3t_in, qkv_in, wt_in, p_in = saved
    pairs = [(n3t_in, n3t), (wt_in, wt), (xh_in, xh), (rs_in, rs), (x3_in, triple.at[:, body]), (dx_in, dx)]
    copies = [pltpu.make_async_copy(src, dst, in_sems.at[i]) for i, (src, dst) in enumerate(pairs)]
    pairs = tiles // 2
    cut = 2 * 2 * TILE
    segments = []
    for half, (top, end) in enumerate(((0, cut), (cut, 2 * pairs * TILE))):
        rows = pl.ds(top, end - top)
        spread = pl.ds(top + 2 * HALO * half, end - top + 2 * HALO * (1 - half))
        arrays = [(qkv_in.at[0], q, rows), (qkv_in.at[1], kp, spread), (qkv_in.at[2], vp, spread)]
        arrays += [(do_in, do, rows), (p_in, p, rows)]
        segments.append(
            [
                pltpu.make_async_copy(src.at[part], dst.at[part], part_sems.at[half, j])
                for j, (src, dst, part) in enumerate(arrays)
            ]
        )
    for copy in segments[0]:
        copy.start()
    if near:
        up_refs, down_refs, early_refs, tail_refs = refs[:12], refs[12:24], refs[24:36], refs[36:]
        core = lax.axis_index("dp") % 2
        loads = [
            pltpu.make_async_copy(src.at[half], refs[0].at[half], in_sems.at[6 + k])
            for k, (src, refs, half) in enumerate(
                (
                    (up_in, up_refs, 1 - core), (down_in, down_refs, 1 - core),
                    (up_in, up_refs, core), (down_in, down_refs, core),
                )
            )
        ]
        loads[0].start()
        loads[1].start()
        greet()
        up_sum, down_sum, early_sum = RelayScatter(*up_refs), RelayScatter(*down_refs), RelayScatter(*early_refs)
        tail = Tail(*tail_refs)
        loads[0].wait()
        up_sum.to_core()
        loads[1].wait()
        down_sum.to_core()
        loads[2].start()
        loads[3].start()
        early_sums = early_refs[0]
    for copy in segments[1]:
        copy.start()
    carry_k[...] = jnp.zeros_like(carry_k)
    carry_v[...] = jnp.zeros_like(carry_v)
    acc[...] = jnp.zeros_like(acc)
    ij = [lax.broadcasted_iota(jnp.int32, unit.shape, k) for k in range(2)]
    unit[...] = (ij[0] == ij[1]).astype(F32).astype(BF16)
    zero8 = jnp.zeros((8, D), F32)
    for j in range(3):
        triple[j, 0:8, :] = zero8
        triple[j, frames + 8 : frames + 16, :] = zero8

    def attend(tile, span):
        heads = [slice(head * HEAD, (head + 1) * HEAD) for head in range(HEADS)]
        probs = [p[tile, cols] for cols in heads]
        d_probs = [mm_nt(do[tile, cols], vp[span, cols]) for cols in heads]
        inner = [jnp.sum(pr * dp, axis=-1, keepdims=True) for pr, dp in zip(probs, d_probs)]
        d_scores = [(pr * (dp - mean)).astype(BF16) for pr, dp, mean in zip(probs, d_probs, inner)]
        turned = [mm_nt(unit[...], pr.astype(BF16)).astype(BF16) for pr in probs]
        dvs = [mm(pr, do[tile, cols]) for pr, cols in zip(turned, heads)]
        dqs = [mm(ds, kp[span, cols]) for ds, cols in zip(d_scores, heads)]
        turned = [mm_nt(unit[...], ds).astype(BF16) for ds in d_scores]
        dks = [mm(ds, q[tile, cols]) for ds, cols in zip(turned, heads)]
        return dqs, dks, dvs

    def attend_step(i, carry):
        @pl.when(i == 2)
        def _():
            for copy in segments[1]:
                copy.wait()

        @pl.when(i == pairs // 4)
        def _():
            if near:
                loads[2].wait()
                up_sum.to_plane()
            for copy in copies[0:4]:
                copy.start()

        @pl.when(i == pairs // 2)
        def _():
            if near:
                loads[3].wait()
                down_sum.to_plane()

        @pl.when(i == pairs - 2)
        def _():
            if near:
                up_sum.relay()
            copies[4].start()

        starts = [pl.multiple_of((2 * i + k) * TILE, 32) for k in range(2)]
        results = [attend(pl.ds(start, TILE), pl.ds(start, SPAN)) for start in starts]
        start = starts[0]
        for head in range(HEADS):
            cols = slice(head * HEAD, (head + 1) * HEAD)
            for which, held, ref in ((1, carry_k, kp), (2, carry_v, vp)):
                one, two = (result[which][head] for result in results)
                ref[pl.ds(start, 32), cols] = (one[0:32] + held[:, cols]).astype(BF16)
                ref[pl.ds(start + 32, TILE - 32), cols] = one[32:TILE].astype(BF16)
                ref[pl.ds(start + TILE, 32), cols] = (one[TILE:SPAN] + two[0:32]).astype(BF16)
                ref[pl.ds(start + TILE + 32, TILE - 32), cols] = two[32:TILE].astype(BF16)
                held[:, cols] = two[TILE:SPAN]
            for k in range(2):
                q[pl.ds(starts[k], TILE), cols] = results[k][0][head].astype(BF16)
        return carry

    for copy in segments[0]:
        copy.wait()
    lax.fori_loop(0, pairs, attend_step, 0)
    if near:
        down_sum.relay()
    copies[5].start()
    copies[0].wait()
    spans = [slice(j * WIDTH, (j + 1) * WIDTH) for j in range(3)]
    deal(early_sums, spans[0], mm(n3t[0], q[0:frames, :]) * FACTOR)
    deal(early_sums, spans[1], mm(n3t[1], kp[HALO : HALO + frames, :]))
    if near:
        up_sum.to_z()
    deal(early_sums, spans[2], mm(n3t[2], vp[HALO : HALO + frames, :]))
    if near:
        early_sum.to_core()
        down_sum.to_z()
    for copy in copies[1:5]:
        copy.wait()

    def add(row, value):
        acc[row] += fold(value)

    def norm_tile(i, carry):
        if near:

            @pl.when(i == steps // 4)
            def _():
                early_sum.to_plane()

            @pl.when(i == steps * 5 // 8)
            def _():
                early_sum.relay()

            @pl.when(i == steps - 1)
            def _():
                early_sum.to_z()

        top = pl.multiple_of(i * ROWS, ROWS)
        padded = pl.ds(top + HALO, ROWS)
        for j, low in enumerate((q[pl.ds(top, ROWS), :], kp[padded, :], vp[padded, :])):
            ups[j] = mm(low, wt[j])

        def step(k, carry):
            return norm_step(top, k, carry)

        return lax.fori_loop(0, ROWS // PAIR, step, carry)

    def norm_step(top, k, carry):
        for s in range(PAIR // SUB):
            offset = pl.multiple_of(k * PAIR + s * SUB, SUB)
            start = pl.multiple_of(top + offset, SUB)
            here, rows, body = pl.ds(offset, SUB), pl.ds(start, SUB), pl.ds(start + 8, SUB)
            lows = {0: q[rows, :], 2: vp[pl.ds(start + HALO, SUB), :]}
            live = (row_index(start) < ends[1]).astype(F32)[:, 0:1]
            not_first, not_last = inside(row_index(start), ends, frames)
            window = xh[pl.ds(start, SUB + 16), :]
            before, own, after = window[7 : SUB + 7], window[8 : SUB + 8], window[9 : SUB + 9]
            spread = [0.0, 0.0, 0.0]
            for j, (gain, taps) in enumerate(((2, 15), (4, 18), (5, 21))):
                upstream = ups[j, here, :]
                gains = vec_ref[gain : gain + 1, :]
                if j == 0:
                    gains = gains * FACTOR
                    add(9, lows[j].astype(F32))
                elif j == 2:
                    add(10, lows[j].astype(F32))
                normal = triple[j, body, :]
                add(gain, upstream * normal)
                if j != 1:
                    add(gain + 1, upstream)
                masked = norm_back(upstream, gains, normal, rs[rows, j : j + 1] * live)
                masked_first, masked_last = masked * not_first, masked * not_last
                add(taps, masked_first * before)
                add(taps + 1, masked * own)
                add(taps + 2, masked_last * after)
                add(taps + 9, masked_first)
                add(taps + 10, masked)
                add(taps + 11, masked_last)
                spread[0] = spread[0] + vec_ref[taps : taps + 1, :] * masked_first
                spread[1] = spread[1] + vec_ref[taps + 1 : taps + 2, :] * masked
                spread[2] = spread[2] + vec_ref[taps + 2 : taps + 3, :] * masked_last
            for tap in range(3):
                triple[tap, body, :] = spread[tap]
        return carry

    steps = frames // ROWS
    lax.fori_loop(0, steps, norm_tile, 0)

    sums = jnp.sum(acc[...], axis=1)
    along, plain, taps = sums[15:24], sums[24:33], vec_ref[15:24, :]
    table = jnp.concatenate(
        [
            total(taps * along),
            total(taps * plain),
            sums[2:4] * FACTOR,
            sums[4:7],
            gmid_ref[0:2, :],
            sums[9:10] * FACTOR,
            sums[10:11],
            gmid_ref[3:5, :],
            gmid_ref[2:3, :],
            gmid_ref[5:6, :],
            vec_ref[0:1, :] * along + vec_ref[1:2, :] * plain,
            gmid_ref[8:12, :],
        ],
        axis=0,
    )
    if near:
        turned = jnp.concatenate([table, jnp.zeros((128 - table.shape[0], D), F32)], axis=0).T
        tail.start(turned)
    else:
        gvec[...] = table
    copies[5].wait()

    early_rows = frames * 3 // 4
    leave = [
        pltpu.make_async_copy(dx.at[rows], ig_out.at[rows], out_sems.at[i])
        for i, rows in enumerate((pl.ds(0, early_rows), pl.ds(early_rows, frames - early_rows)))
    ]

    def input_step(i, carry):
        if near:

            @pl.when(i == frames // PAIR // 4)
            def _():
                up_sum.finish()

            @pl.when(i == frames // PAIR * 3 // 4)
            def _():
                down_sum.finish()

        @pl.when(i == early_rows // PAIR)
        def _():
            leave[0].start()

        for s in range(PAIR // SUB):
            start = pl.multiple_of(i * PAIR + s * SUB, SUB)
            rows = pl.ds(start, SUB)
            live = live_rows(start, ends)
            later = triple[0, pl.ds(start + 8, SUB + 8), :][1 : SUB + 1]
            earlier = triple[2, pl.ds(start, SUB + 8), :][7 : SUB + 7]
            d_normed = triple[1, pl.ds(start + 8, SUB), :] + later + earlier
            normal = xh[pl.ds(start + 8, SUB), :]
            dx[rows, :] = live * dx[rows, :] + norm_back(d_normed, vec_ref[0:1, :], normal, rs[rows, 3:4])
        return carry

    lax.fori_loop(0, frames // PAIR, input_step, 0)
    leave[1].start()
    if near:
        up_part[...] = up_sum.result[...]
        down_part[...] = down_sum.result[...]
        early_sum.finish()
        early_part[...] = early_sum.result[...]
        lanes = 0.0
        for ref in (early_part, up_part, down_part):
            squares = total(ref[...] * ref[...])
            lanes = lanes + sum(squares[:, c * 128 : (c + 1) * 128] for c in range(D // 128))
        tail.along_z(lanes)
        vec_part[...], lanes = tail.finish()
        square[...] = jnp.broadcast_to(jnp.sum(lanes, axis=1, keepdims=True), (8, 128))
        for part in (up_sum, down_sum, early_sum, tail):
            part.sent_all()
    for copy in leave:
        copy.wait()


def back(near, lengths, vectors, sums_middle, later_sums, saved, do, dx):
    frames = dx.shape[0]
    half = D // WIDTH // 2
    dma = pltpu.SemaphoreType.DMA
    rows = 3 * WIDTH
    outs = [((frames, D), F32)]
    if near:
        outs += [((rows, D), F32), ((UP, D), F32), ((DOWN, D), F32), ((WIDTH, 128), F32), ((8, 128), F32)]
    else:
        outs += [((2, half, rows, D), F32), ((28, D), F32)]
    scratch = [(array.shape, array.dtype) for array in saved[2:]]
    scratch += [
        ((frames + 16, D), F32),
        ((3, frames + 16, D), F32),
        (do.shape, BF16),
        ((32, D), F32),
        ((32, D), F32),
        ((33, 8, D), F32),
        ((SPAN, HEAD), BF16),
        ((3, ROWS, D), F32),
    ]
    scratch = [pltpu.VMEM(shape, kind) for shape, kind in scratch] + [dma((10,)), dma((2, 5)), dma((2,))]
    params = dict(vmem_limit_bytes=VMEM_LIMIT)
    if near:
        scratch += RelayScatter.scratch(UP, D) + RelayScatter.scratch(DOWN, D) + RelayScatter.scratch(rows, D)
        scratch += Tail.scratch()
        params.update(collective_id=1, has_side_effects=True)
    else:
        later_sums = ()
    return pl.pallas_call(
        functools.partial(back_kernel, near),
        out_shape=[jax.ShapeDtypeStruct(shape, kind) for shape, kind in outs],
        in_specs=[IN_SMEM, IN_VMEM, IN_VMEM] + [ANY] * (len(later_sums) + len(saved) + 2),
        out_specs=[ANY] + [IN_VMEM] * (len(outs) - 1),
        scratch_shapes=scratch,
        compiler_params=pltpu.CompilerParams(**params),
        name="back",
    )(lengths, vectors, sums_middle, *later_sums, *saved, do, dx)


MESH = pl.DeviceIdType.MESH
PLANE = ((0, 1), (1, 0), (1, 1))
WIDTH = 16
UP = 5 * WIDTH
DOWN = 4 * WIDTH


def place():
    me = lax.axis_index("dp")
    return me // 8, (me // 4) % 2, (me // 2) % 2, me % 2


def index_of(z, y, x, core):
    return ((z * 2 + y) * 2 + x) * 2 + core


def plane_partner(step):
    z, y, x, core = place()
    return index_of(z, (y + step[0]) % 2, (x + step[1]) % 2, core)


def core_partner():
    z, y, x, core = place()
    return index_of(z, y, x, 1 - core)


def z_partner(step):
    z, y, x, core = place()
    return index_of((z + step) % 4, y, x, core)


def remote(src, dst, send_sem, recv_sem, device):
    return pltpu.make_async_remote_copy(
        src_ref=src, dst_ref=dst, send_sem=send_sem, recv_sem=recv_sem, device_id=(device,), device_id_type=MESH
    )


def flat_place():
    z, y, x, core = place()
    return (core * 2 + y) * 2 + x


def flat_partner(k):
    spot = (flat_place() + k) % 8
    return spot, index_of(place()[0], spot // 2 % 2, spot % 2, spot // 4)


def near_partners():
    return [z_partner(step) for step in (1, 2, 3)] + [flat_partner(k)[1] for k in range(1, 8)]


def greet():
    barrier = pltpu.get_barrier_semaphore()
    partners = near_partners()
    for partner in partners:
        pl.semaphore_signal(barrier, inc=1, device_id=(partner,), device_id_type=MESH)
    pl.semaphore_wait(barrier, len(partners))


def arrived(part, sem):
    remote(part, part, sem, sem, core_partner()).wait_recv()


def left(part, sem):
    remote(part, part, sem, sem, core_partner()).wait_send()


class Tail:
    def __init__(self, columns, inbox, z_out, z_box, norm_box, sems):
        self.columns, self.inbox, self.z_out, self.z_box, self.norm_box = columns, inbox, z_out, z_box, norm_box
        self.sems = sems

    @staticmethod
    def scratch():
        shapes = [(8, WIDTH, 128), (8, WIDTH, 128), (WIDTH + 8, 128), (4, WIDTH + 8, 128), (8, 8, 128)]
        return [pltpu.VMEM(shape, F32) for shape in shapes] + [pltpu.SemaphoreType.DMA((6,))]

    def send(self, k, src, dst, device):
        remote(src, dst, self.sems.at[3 + k], self.sems.at[k], device).start()

    def start(self, turned):
        for spot in range(8):
            tile = 0.0
            for z in range(4):
                owner = ((z * 2 + spot // 2 % 2) * 2 + spot % 2) * 2 + spot // 4
                part = turned[owner * WIDTH : (owner + 1) * WIDTH]
                tile = tile + (pltpu.roll(part, 32 * z, 1) if z else part)
            self.columns[spot] = tile
        own = flat_place()
        self.inbox[own] = self.columns[own]
        for k in range(1, 8):
            spot, device = flat_partner(k)
            self.send(0, self.columns.at[spot], self.inbox.at[own], device)

    def along_z(self, squares):
        z = place()[0]
        arrived(self.inbox.at[pl.ds(0, 7)], self.sems.at[0])
        self.z_out[0:WIDTH, :] = jnp.sum(self.inbox[...], axis=0)
        self.z_out[WIDTH:, :] = jnp.broadcast_to(squares, (8, 128))
        self.z_box[z] = self.z_out[...]
        for k in range(3):
            self.send(1, self.z_out, self.z_box.at[z], z_partner(k + 1))

    def finish(self):
        z, own = place()[0], flat_place()
        arrived(self.z_box.at[pl.ds(0, 3)], self.sems.at[1])
        whole = jnp.sum(self.z_box[...], axis=0)
        column = whole[0:WIDTH]
        squares = total(column * column) + whole[WIDTH : WIDTH + 1]
        self.norm_box[own] = jnp.broadcast_to(squares, (8, 128))
        for k in range(1, 8):
            self.send(2, self.norm_box.at[own], self.norm_box.at[own], flat_partner(k)[1])
        part = jnp.where(z == 0, column, 0.0)
        for k in range(1, 4):
            part = part + jnp.where(z == k, pltpu.roll(column, 128 - 32 * k, 1), 0.0)
        arrived(self.norm_box.at[pl.ds(0, 7)], self.sems.at[2])
        return part, jnp.sum(self.norm_box[...], axis=0)

    def sent_all(self):
        for k, part in enumerate((self.inbox.at[pl.ds(0, 7)], self.z_box.at[pl.ds(0, 3)], self.norm_box.at[pl.ds(0, 7)])):
            left(part, self.sems.at[3 + k])


class Gather:
    def __init__(self, slots, sems):
        self.slots, self.sems = slots, sems

    def slot(self):
        z, y, x, core = place()
        return self.slots.at[((core * 2 + y) * 2 + x) * 4 + z]

    def column(self, step=(0, 0), start=0, size=4):
        z, y, x, core = place()
        base = ((core * 2 + (y + step[0]) % 2) * 2 + (x + step[1]) % 2) * 4
        return self.slots.at[pl.ds(base + start, size)]

    def send(self, k, part, device):
        remote(part, part, self.sems.at[5], self.sems.at[k], device).start()

    def wait(self, k, size):
        arrived(self.slots.at[pl.ds(0, size)], self.sems.at[k])

    def start_z(self):
        for k in range(3):
            self.send(0, self.slot(), z_partner(k + 1))

    def along_z(self):
        self.wait(0, 3)
        own = self.column()
        for k in range(2):
            self.send(1 + k, own, plane_partner(PLANE[k]))
        self.send(4, own, core_partner())

    def in_plane(self):
        for k in range(2):
            self.wait(1 + k, 4)
            self.send(3, self.column(PLANE[k], start=2 * k, size=2), plane_partner(PLANE[1 - k]))
            self.send(4, self.column(PLANE[k]), core_partner())

    def diagonal(self):
        self.wait(3, 4)
        self.send(4, self.column(PLANE[2]), core_partner())

    def all_along_z(self):
        self.wait(0, 3)
        for k in range(1, 8):
            self.send(1, self.column(), flat_partner(k)[1])

    def all_arrive(self):
        self.wait(1, 28)

    def arrive(self):
        self.wait(4, 16)

    def sent_all(self):
        left(self.slots.at[pl.ds(0, 31)], self.sems.at[5])


class RelayScatter:
    def __init__(self, sums, core_in, ahead_out, ahead_in, after_out, after_in, z_out, z_in, held, whole, *rest):
        self.sums, self.core_in = sums, core_in
        self.ahead_out, self.ahead_in, self.after_out, self.after_in = ahead_out, ahead_in, after_out, after_in
        self.z_out, self.z_in, self.held, self.whole = z_out, z_in, held, whole
        self.result, self.sems = rest

    @staticmethod
    def scratch(rows, lanes):
        counts = [(2, 16), (16,), (2, 4), (2, 4), (2, 2), (2, 2), (3,), (3,), (4,)]
        return (
            [pltpu.VMEM((*count, rows, lanes), BF16) for count in counts]
            + [pltpu.VMEM((4, rows, lanes), F32), pltpu.VMEM((rows, lanes), F32)]
            + [pltpu.SemaphoreType.DMA((8,))]
        )

    def send(self, k, src, dst, device):
        remote(src, dst, self.sems.at[4 + k], self.sems.at[k], device).start()

    def blocks(self, work):
        def step(r, carry):
            work(pl.ds(pl.multiple_of(r * WIDTH, WIDTH), WIDTH))
            return carry

        lax.fori_loop(0, self.result.shape[0] // WIDTH, step, 0)

    def to_core(self):
        self.send(0, self.sums.at[1 - place()[3]], self.core_in, core_partner())

    def to_plane(self):
        arrived(self.core_in, self.sems.at[0])
        z, y, x, core = place()

        def both(step, zz, rows):
            chip = ((y + step[0]) % 2 * 2 + (x + step[1]) % 2) * 4 + zz
            return self.sums[core, chip, rows, :] + self.core_in[chip, rows, :]

        for k in range(2):

            def pack(rows):
                for half in range(2):
                    self.ahead_out[k, half, rows, :] = both(PLANE[2], 2 * k + half, rows)
                    self.ahead_out[k, 2 + half, rows, :] = both(PLANE[k], 2 * k + half, rows)

            self.blocks(pack)
            self.send(1, self.ahead_out.at[k], self.ahead_in.at[k], plane_partner(PLANE[k]))

        def keep(rows):
            for k in range(2):
                for half in range(2):
                    self.after_out[k, half, rows, :] = both(PLANE[k], 2 * (1 - k) + half, rows)
                    self.held[2 * k + half, rows, :] = both((0, 0), 2 * k + half, rows)

        self.blocks(keep)

    def relay(self):
        arrived(self.ahead_in, self.sems.at[1])
        for k in range(2):

            def pack(rows):
                for half in range(2):
                    at = (k, half, rows, slice(None))
                    self.after_out[at] = self.after_out[at] + self.ahead_in[1 - k, half, rows, :]

            self.blocks(pack)
            self.send(2, self.after_out.at[k], self.after_in.at[k], plane_partner(PLANE[k]))

    def to_z(self):
        z, y, x, core = place()
        arrived(self.after_in, self.sems.at[2])

        def add(rows):
            for k in range(2):
                for half in range(2):
                    value = self.held[2 * k + half, rows, :].astype(F32) + self.ahead_in[k, 2 + half, rows, :].astype(F32)
                    self.whole[2 * k + half, rows, :] = value + self.after_in[1 - k, half, rows, :].astype(F32)

        self.blocks(add)

        def pack(rows):
            for k in range(3):
                self.z_out[k, rows, :] = self.whole[(z + k + 1) % 4, rows, :].astype(BF16)
            self.result[rows, :] = self.whole[z, rows, :]

        self.blocks(pack)
        for k in range(3):
            self.send(3, self.z_out.at[k], self.z_in.at[k], z_partner(k + 1))

    def finish(self):
        arrived(self.z_in, self.sems.at[3])

        def add(rows):
            value = self.result[rows, :]
            for k in range(3):
                value = value + self.z_in[k, rows, :].astype(F32)
            self.result[rows, :] = value

        self.blocks(add)

    def sent_all(self):
        for k, part in enumerate((self.core_in, self.ahead_in, self.after_in, self.z_in)):
            left(part, self.sems.at[4 + k])


def update_kernel(len_ref, ig_in, early_part, up_part, down_part, vec_part, square, *refs):
    state_in, norm_out, bias_out, refs = refs[:16], refs[16], refs[17], refs[18:]
    state_out, ig_out, state, new, refs = refs[:16], refs[16], refs[17:33], refs[33:49], refs[49:]
    passing, state_sems, new_sems, in_sems, out_sems = refs
    pieces = in_sems.shape[0]
    size = ig_in.shape[0] // pieces
    parts = [slice(i * size, (i + 1) * size) for i in range(pieces)]
    loads = copy_all(zip(state_in, state), state_sems)
    ig_loads = copy_all([(ig_in.at[part], passing.at[part]) for part in parts], in_sems)
    ig_stores = [
        pltpu.make_async_copy(passing.at[part], ig_out.at[part], out_sems.at[i]) for i, part in enumerate(parts)
    ]
    stores = [pltpu.make_async_copy(new[i], state_out[i], new_sems.at[i]) for i in range(16)]
    n = len_ref.shape[1]
    live = lax.fori_loop(0, n, lambda i, count: count + len_ref[0, i] + len_ref[1, i], jnp.int32(0))
    share = 1.0 / jnp.full((8, 128), live, jnp.int32).astype(F32)
    norm = jnp.sqrt(square[...]) * share
    limit = 0.03 * math.sqrt(NPARAM / (n * FRAMES_DEV))
    factor = (limit / jnp.maximum(norm, limit) * share)[0:1, 0:1]
    norm_out[...] = norm[0:1, 0:1]
    turned = jnp.concatenate([vec_part[...], jnp.zeros((128 - WIDTH, 128), F32)], axis=0).T
    bias_out[...] = turned[12:13, 0:WIDTH] * factor

    def apply(gradient, which, at, rate):
        weight, one, two, average = (state[4 * which + j][at] for j in range(4))
        result = adamw(gradient * factor, weight, one, two, average, rate)
        for j in range(4):
            new[4 * which + j][at] = result[j]

    for which in range(4):
        for load in loads[4 * which : 4 * which + 4]:
            load.wait()
        if which == 0:
            for j in range(3):
                apply(early_part[j * WIDTH : (j + 1) * WIDTH, :], 0, j, 0.05)
            apply(up_part[0:WIDTH, :], 0, 3, 0.05)
        elif which == 1:
            for c in range(FF // D):
                at = (slice(None), slice(c * D, (c + 1) * D))
                apply(up_part[(1 + c) * WIDTH : (2 + c) * WIDTH, :], 1, at, 0.05)
        elif which == 2:
            apply(down_part[...], 2, slice(None), 0.05)
        else:
            apply(vec_part[:, 0 : state[12].shape[1]], 3, slice(None), 0.25)
        for store in stores[4 * which : 4 * which + 4]:
            store.start()
        for i in range(which * pieces // 4, (which + 1) * pieces // 4):
            ig_loads[i].wait()
            ig_stores[i].start()
    for store in stores + ig_stores:
        store.wait()


def update(lengths, input_grad, parts, state):
    small = [jax.ShapeDtypeStruct(shape, F32) for shape in ((1, 1), (1, WIDTH))]
    large = [jax.ShapeDtypeStruct(array.shape, F32) for array in (*state, input_grad)]
    dma = pltpu.SemaphoreType.DMA
    results = pl.pallas_call(
        update_kernel,
        out_shape=small + large,
        in_specs=[IN_SMEM, ANY] + [IN_VMEM] * len(parts) + [ANY] * len(state),
        out_specs=[IN_VMEM] * 2 + [ANY] * len(large),
        scratch_shapes=[pltpu.VMEM(array.shape, F32) for array in (*state, *state, input_grad)]
        + [dma((16,)), dma((16,)), dma((4,)), dma((4,))],
        compiler_params=pltpu.CompilerParams(vmem_limit_bytes=VMEM_LIMIT),
        name="update",
    )(lengths, input_grad, *parts, *state)
    return (*results[2:18], results[0], results[1], results[18])


def adamw(gradient, weight, moment_one, moment_two, average, rate):
    new_one = 0.9 * moment_one + 0.1 * gradient
    new_two = 0.999 * moment_two + 0.001 * gradient * gradient
    corrected = new_one / (1.0 - 0.9**STEP)
    spread = jnp.sqrt(new_two / (1.0 - 0.999**STEP)) + 1e-08
    new_weight = weight - rate * (corrected / spread + 0.1 * weight)
    new_average = 0.9 * average + 0.1 * new_weight
    return (new_weight, new_one, new_two, new_average)


def to_slots(array):
    array = array.reshape(4, 2, 2, 2, *array.shape[1:])
    return array.transpose(3, 1, 2, 0, *range(4, array.ndim)).reshape(-1, *array.shape[4:])


def to_owners(array):
    array = array.reshape(2, 2, 2, 4, *array.shape[2:])
    return array.transpose(3, 1, 2, 0, *range(4, array.ndim)).reshape(-1, *array.shape[4:])


def pack_weights(mixes, up, down, vectors):
    owners = D // WIDTH
    table = jnp.pad(vectors.T, ((0, 0), (0, D - vectors.shape[0])))
    early = [matrix.reshape(owners, WIDTH, D) for matrix in (mixes[0], mixes[1], mixes[2], table)]
    later = [matrix.reshape(owners, WIDTH, D) for matrix in (mixes[3], *jnp.split(up, FF // D, axis=1))]
    slots = (jnp.concatenate(early, axis=1), jnp.concatenate(later, axis=1), down.reshape(owners, DOWN, D))
    return tuple(to_slots(array) for array in slots)


def body(
    activations,
    cotangent,
    video_length,
    mix_weight,
    mix_first,
    mix_second,
    mix_average,
    up_weight,
    up_first,
    up_second,
    up_average,
    down_weight,
    down_first,
    down_second,
    down_average,
    vector_weight,
    vector_first,
    vector_second,
    vector_average,
):
    groups = lax.axis_size("dp")
    near = groups == 32
    lengths = video_length.T
    if near:
        weights = (mix_weight, up_weight, down_weight, vector_weight.T)
        vectors, up, down, *saved = front(near, lengths, activations, weights)
    else:
        early, up, down = pack_weights(
            lax.all_gather(mix_weight.astype(BF16), "dp", axis=1, tiled=True),
            lax.all_gather(up_weight.astype(BF16), "dp", axis=0, tiled=True),
            lax.all_gather(down_weight.astype(BF16), "dp", axis=0, tiled=True),
            lax.all_gather(vector_weight.astype(BF16), "dp", axis=1, tiled=True),
        )
        vectors, *saved = front(near, lengths, activations, (early,))
    attended = saved.pop()
    block_output, d_middle, d_attended, *later_sums, sums_middle = middle(
        near, lengths, attended, activations, cotangent, vectors, up, down
    )
    input_grad, *sums = back(near, lengths, vectors, sums_middle, later_sums, saved, d_attended, d_middle)
    if near:
        state = (
            mix_weight, mix_first, mix_second, mix_average, up_weight, up_first, up_second, up_average,
            down_weight, down_first, down_second, down_average,
            vector_weight.T, vector_first.T, vector_second.T, vector_average.T,
        )
        *new_state, grad_norm, clipped, input_grad = update(lengths, input_grad, sums, state)
        new_state[12:] = [array.T for array in new_state[12:]]
        return (block_output, input_grad, grad_norm.reshape(()), *new_state, clipped.reshape(-1))
    early_sum = to_owners(sums[0]).reshape(-1, 3, WIDTH, D)
    up_sum, down_sum = (to_owners(array) for array in later_sums)
    vector_grad = sums[1]
    mix_grad = jnp.stack(
        [early_sum[:, j].reshape(D, D) for j in range(3)] + [up_sum[:, 0:WIDTH].reshape(D, D)]
    )
    grad_up = jnp.concatenate(
        [up_sum[:, (c + 1) * WIDTH : (c + 2) * WIDTH].reshape(D, D) for c in range(FF // D)], axis=1
    )
    grad_down = down_sum.reshape(FF, D)
    live_total = jnp.sum(video_length).astype(F32)
    mix_part = lax.psum_scatter(mix_grad, "dp", scatter_dimension=1, tiled=True) / live_total
    up_part = lax.psum_scatter(grad_up, "dp", scatter_dimension=0, tiled=True) / live_total
    down_part = lax.psum_scatter(grad_down, "dp", scatter_dimension=0, tiled=True) / live_total
    vector_part = lax.psum_scatter(vector_grad, "dp", scatter_dimension=1, tiled=True) / live_total
    square_sum = lax.psum(
        jnp.sum(mix_part * mix_part)
        + jnp.sum(up_part * up_part)
        + jnp.sum(down_part * down_part)
        + jnp.sum(vector_part * vector_part),
        "dp",
    )
    grad_norm = jnp.sqrt(square_sum)
    clip_limit = 0.03 * math.sqrt(NPARAM / (groups * FRAMES_DEV))
    clip_factor = clip_limit / jnp.maximum(grad_norm, clip_limit)
    mix_new = adamw(mix_part * clip_factor, mix_weight, mix_first, mix_second, mix_average, 0.05)
    up_new = adamw(up_part * clip_factor, up_weight, up_first, up_second, up_average, 0.05)
    down_new = adamw(
        down_part * clip_factor, down_weight, down_first, down_second, down_average, 0.05
    )
    vector_new = adamw(
        vector_part * clip_factor, vector_weight, vector_first, vector_second, vector_average, 0.25
    )
    clipped_bias_grad = vector_part[12] * clip_factor
    return (
        block_output,
        input_grad,
        grad_norm,
        *mix_new,
        *up_new,
        *down_new,
        *vector_new,
        clipped_bias_grad,
    )


def solution(mesh):
    state = [P(None, "dp", None)] * 4 + [P("dp", None)] * 8 + [P(None, "dp")] * 4
    rows = P("dp", None)
    return jax.shard_map(
        body,
        mesh=mesh,
        in_specs=(rows, rows, P(), *state),
        out_specs=(rows, rows, P(), *state, P("dp")),
        check_vma=False,
    )
```

time: 807 us -> 169 us (0.21)
  matrix products: 257 us -> 0 us
  Pallas kernels: 0 us -> 168 us
  local copies, waits for them, and re-layouts: 144 us -> 0 us
  waiting for transfers between devices: 135 us -> 0 us
  other arithmetic: 123 us -> 0 us
  blocking collectives: 83.9 us -> 0 us
  loops' own time: 36.9 us -> 0 us
  between operations: 19.9 us -> 0.84 us
    dot_general x46 -> x0, matrix products: 257 us -> none  [the longest x1 46.6 us: body(): jnp.dot(normed_low, up_full, preferred_element_type=jnp.float32)]
    pallas_call x0 -> x4, Pallas kernels: none -> 168 us  [the longest x1 63.3 us: back(): pl.pallas_call(functools.partial(back_kernel, near), out_shape=[jax.Shape...]
    psum x1 -> x0, waiting for transfers between devices: 134 us -> none  [body(): lax.psum((mix_grad, grad_up, grad_down, vector_grad), 'dp')]
    reduce_sum x24 -> x0, other arithmetic: 63.6 us -> none  [the longest x1 16.3 us: conv_back(): jnp.sum(masked * before, axis=0)]
    dynamic_update_slice x8 -> x0, local copies, waits for them, and re-layouts: 48.5 us -> none  [the longest x4 24.3 us: attend_back(): lax.dynamic_update_slice_in_dim(value_acc, lax.dynamic_slice_in_dim(value...]
    all_gather x1 -> x0, blocking collectives: 43.6 us -> none  [body(): lax.all_gather(vector_weight.astype(jnp.bfloat16), 'dp', axis=1, tiled=True)]
    psum x1 -> x0, blocking collectives: 40.4 us -> none  [body(): lax.psum((mix_grad, grad_up, grad_down, vector_grad), 'dp')]
    another operation x2 -> x0, loops' own time: 36.9 us -> none  [the longest x1 18.6 us: body(): lax.scan(attend_back, (zeros_pad, zeros_pad), (starts, log_totals))]
  transfers between devices with their start and end apart: 4 -> 0, of which waited for: 1 -> 0; matrix products, arithmetic and copies ran while one was open for 26% -> 0% of each run, Pallas kernels for 0% -> 0%
where the time goes in v1:
time: 169 us
  Pallas kernels  168 us (99%)
    pallas_call x1, Pallas kernels, back(): pl.pallas_call(functools.partial(back_kernel, near), out_shape=[jax.Shape...  63.3 us
    pallas_call x1, Pallas kernels, front(): pl.pallas_call(functools.partial(front_kernel, near), out_shape=[jax.Shap...  53.8 us
    pallas_call x1, Pallas kernels, middle(): pl.pallas_call(middle_kernel, out_shape=[jax.ShapeDtypeStruct(shape, kind...  44.5 us
    pallas_call x1, Pallas kernels, update(): pl.pallas_call(update_kernel, out_shape=small + large, in_specs=[IN_SMEM,...  6.45 us

profile of v1, /device:TPU:0, one launch (start us, length us, event | category | flops | bytes accessed | tf_op | source)
XLA Modules:
  0.0 168.8 jit_solution(4105101160864138359)
XLA Ops:
  0.7 53.8 %front.1 = (f32[32,512]{1,0:T(8,128)}, bf16[32,80,512]{2,1,0:T(8,128)(2,1)}, bf16[32,64,512]{2,1,0:T(8,128)(2,1)}, f32[2064,512]{1,0:T(8,128)}, f32[3,2048,512]{...) custom-call(s32[2,32]{1,0:T(2,128)} %bitcast.13, ...), custom_call_target="tpu_custom_call" | custom-call | tf_op jit(solution)/shard_map/front/pallas_call | solution.py:353
  54.4 44.5 %middle.1 = (bf16[2048,512]{1,0:T(8,128)(2,1)}, f32[2048,512]{1,0:T(8,128)}, bf16[2112,512]{1,0:T(8,128)(2,1)}, bf16[2,16,80,512]{3,2,1,0:T(8,128)(2,1)}, bf16[2...) custom-call(s32[2,32]{1,0:T(2,128)} %bitcast.14, bf16[2112,512]{1,0:T(8,128)(2,1)} %get-tuple-element.62.o_in, ...), custom_call_target="tpu_custom_call" | custom-call | tf_op jit(solution)/shard_map/middle/pallas_call | solution.py:597
  98.9 63.3 %back.1 = (f32[2048,512]{1,0:T(8,128)}, f32[48,512]{1,0:T(8,128)}, f32[80,512]{1,0:T(8,128)}, f32[64,512]{1,0:T(8,128)}, f32[16,128]{1,0:T(8,128)}, /*index=5*/f32[8,128]{1,0:T(8,128)}) custom-call(s32[2,32]{1,0:T(2,128)} %bitcast.15, f32[32,512]{1,0:T(8,128)} %get-tuple-element.63.vec_ref, f32[16,512]{1,0:T(8,128)} %get-tuple-element.67.gmid_ref, ...), custom_call_target="tpu_custom_call" | custom-call | tf_op jit(solution)/shard_map/back/pallas_call | solution.py:931
  162.2 6.4 %update.1 = (f32[1,1]{1,0:T(1,128)}, f32[1,16]{1,0:T(1,128)}, f32[4,16,512]{2,1,0:T(8,128)}, f32[4,16,512]{2,1,0:T(8,128)}, f32[4,16,512]{2,1,0:T(8,128)}, /*ind...) custom-call(s32[2,32]{1,0:T(2,128)} %bitcast.16, ...), custom_call_target="tpu_custom_call" | custom-call | tf_op jit(solution)/shard_map/update/pallas_call | solution.py:1281
